TPU v7x, 256 devices: a whole 4x4x8 slice. The times are simulated.
256 devices in a mesh: ch: 64 (over z, y, core), sp: 4 (over x).
Axes of the slice: x: 4, y: 4, z: 8, core: 2. Of those that a mesh axis runs over, the one named last changes fastest.
Arguments:
- volume: bfloat16 [256, 20, 64, 128], P('ch', 'sp'), may hold values from -6 to 6
- weight: bfloat16 [256, 27, 256], P('ch'), may hold values from -0.078125 to 0.078125
- channel_bias: bfloat16 [256], P('ch'), may hold values from -3 to 3
Outputs:
- activated: bfloat16 [256, 20, 64, 128], P('ch', 'sp')
All inputs are finite; a program needn't handle non-finite values.
Results may differ from a plain program's by a relative error of at most 0.0012.
Values may be sent and summed in bfloat16 or wider, within the bound.
A program may use at most 192 MiB of HBM per device.

v0:
```python
import jax
import jax.numpy as jnp
from jax import lax
from jax.sharding import PartitionSpec as P


def extended(cells, sides, width):
    for axis, dim in sides:
        count = lax.axis_size(axis)
        ends = count - 1
        head = lax.slice_in_dim(cells, 0, width, axis=dim)
        tail = lax.slice_in_dim(cells, cells.shape[dim] - width, cells.shape[dim], axis=dim)
        cells = jnp.concatenate(
            [
                lax.ppermute(tail, axis, [(i, (i + 1) % count) for i in range(ends)]),
                cells,
                lax.ppermute(head, axis, [((i + 1) % count, i) for i in range(ends)]),
            ],
            axis=dim,
        )
    return cells


def convolve(portion, filters, edge_pad):
    outer = filters.shape[0]
    inner = filters.shape[2]
    kernel = filters.reshape(outer, 3, 3, 3, inner).transpose(0, 4, 1, 2, 3)
    return lax.conv_general_dilated(
        portion[None],
        kernel,
        (1, 1, 1),
        edge_pad,
        dimension_numbers=("NCDHW", "OIDHW", "NCDHW"),
        preferred_element_type=jnp.float32,
    )[0]


def finish(conv, biases):
    total = conv + biases.astype(jnp.float32)[:, None, None, None]
    return jnp.where(total > 0, total, 0.3 * total).astype(jnp.bfloat16)


def shards(volume, weight, channel_bias):
    columns = lax.all_to_all(volume, "ch", split_axis=2, concat_axis=0, tiled=True)
    framed = extended(columns, (("ch", 2), ("sp", 1)), 1)
    filters, biases = (
        lax.all_gather(weight, "ch", axis=0, tiled=True),
        lax.all_gather(channel_bias, "ch", axis=0, tiled=True),
    )
    conv = convolve(framed, filters, ((0, 0), (0, 0), (1, 1)))
    result = finish(conv, biases)
    return lax.all_to_all(result, "ch", split_axis=0, concat_axis=2, tiled=True)


def solution(mesh):
    return jax.shard_map(
        shards,
        mesh=mesh,
        in_specs=(P("ch", "sp", None, None), P("ch", None, None), P("ch")),
        out_specs=P("ch", "sp", None, None),
        check_vma=False,
    )
```

profile of v0, /device:TPU:2, one launch (start us, length us, event | category | flops | bytes accessed | tf_op | source)
XLA Modules:
  0.0 229.4 jit_solution(4883798582900623747)
XLA Ops:
  6.5 0.0 all-gather.2.cloned.1.call-start
  6.5 1.5 copy.27
  8.0 0.0 all-gather.2.cloned.1.call-update
  8.0 1.2 copy.22
  9.2 0.0 copy-start.1
  9.2 0.0 copy-start
  9.3 30.3 %all_to_all.36 = bf16[4,5,64,128]{3,1,0,2:T(8,128)(2,1)S(1)} all-to-all(bf16[4,5,64,128]{3,1,0,2:T(8,128)(2,1)S(1)} %copy.22), channel_id=1, replica_groups=mesh['ch'=64,'sp'=4] {'ch'}, dimensions={2} | all-to-all | bytes 655360 | tf_op jit(solution)/shard_map/all_to_all | solution.py:44
  39.6 0.1 copy.23
  39.7 1.3 collective-permute-start.1
  41.0 3.1 %collective-permute-start = (bf16[256,5,1,128]{3,0,1,2:T(8,128)(2,1)S(1)}, bf16[256,5,1,128]{3,0,1,2:T(8,128)(2,1)S(1)}, u32[]{:S(2)}, u32[]{:S(2)}) collective-permute-start(bf16[256,5,1,128]{3,0,1,2:T(8,128)(2,1)S(1)} %bitcast.32), channel_id=1, source_target_pairs={{0,4},{4,8},{8,12},{12,16},{16,20},{20,24},{24,28},{28,32},{32,36}... | collective-permute-start | bytes 983048 | tf_op jit(solution)/shard_map/ppermute | solution.py:15
  44.1 0.0 collective-permute-done.1
  44.1 1.2 collective-permute-done
  45.4 2.4 %collective-permute-start.3 = (bf16[256,1,3,128]{3,0,1,2:T(8,128)(2,1)S(1)}, bf16[256,1,3,128]{3,0,1,2:T(8,128)(2,1)S(1)}, u32[]{:S(2)}, u32[]{:S(2)}) collective-permute-start(bf16[256,1,3,128]{3,0,1,2:T(8,128)(2,1)S(1)} %get-tuple-element.6), channel_id=1, source_target_pairs={{1,0},{2,1},{3,2},{5,4},{6,5},{7,6},{9,8},{10,9},{11,10},{13,12},{... | collective-permute-start | bytes 589832 | tf_op jit(solution)/shard_map/ppermute | solution.py:17
  47.8 3.4 %collective-permute-start.2 = (bf16[256,1,3,128]{3,0,1,2:T(8,128)(2,1)S(1)}, bf16[256,1,3,128]{3,0,1,2:T(8,128)(2,1)S(1)}, u32[]{:S(2)}, u32[]{:S(2)}) collective-permute-start(bf16[256,1,3,128]{3,0,1,2:T(8,128)(2,1)S(1)} %get-tuple-element.5), channel_id=1, source_target_pairs={{0,1},{1,2},{2,3},{4,5},{5,6},{6,7},{8,9},{9,10},{10,11},{12,13},{... | collective-permute-start | bytes 589832 | tf_op jit(solution)/shard_map/ppermute | solution.py:15
  51.2 0.0 copy-done.1
  51.2 0.6 dynamic-slice
  52.5 0.0 copy-done
  52.5 0.2 dynamic-update-slice
  52.7 128.0 %all-reduce = bf16[256]{0:T(256)(128)(2,1)S(1)} all-reduce(bf16[256]{0:T(256)(128)(2,1)S(1)} %dynamic-update-slice), channel_id=1, replica_groups=mesh['ch'=64,'sp'=4] {'ch'}, use_global_device_ids=true, to_apply=%add | all-reduce | flops 256 | bytes 1024
  180.7 0.0 collective-permute-done.3
  180.7 0.0 collective-permute-done.2
  180.7 0.2 maximum_bitcast_fusion
  180.9 1.1 copy.33
  182.0 0.3 pad.clone
  182.3 0.3 copy.26
  182.7 0.0 copy-start.2
  182.7 0.0 all-gather.2.cloned.1.call-done
  182.7 4.3 %copy.28 = bf16[256,27,256]{2,0,1:T(8,128)(2,1)S(1)} copy(bf16[256,27,256]{2,1,0:T(8,128)(2,1)} %all-gather.2.cloned.1.call-done) | data formatting | bytes 7077888 | tf_op jit(solution)/shard_map/all_gather | solution.py:47
  187.0 0.0 copy-done.2
  187.0 2.7 %fusion.8 = f32[5,1,8,17,256]{4,2,3,1,0:T(8,128)S(1)} fusion(bf16[256,3,3,3,256]{4,0,3,2,1:T(8,128)(2,1)S(1)} %bitcast.30, bf16[256,7,3,1,7,2]{0,4,5,2,1,3:T(8,128)(2,1)S(1)} %slice.10, bf16[256,7,3,1,8,17]{0,4,5,2,1,3:T(8,128)(2,1)S(1)} %copy.26, pred[8,17]{0,1:T(8,128)(4,1)S(1)} %copy-done.2), kind=kOutput, calls=%fused_computation.10 | convolution fusion | flops 2411558912 | bytes 5848200 | tf_op jit(solution)/shard_map/conv_general_dilated | solution.py:28
  189.7 0.7 copy.29
  190.4 0.9 fusion.12
  191.3 0.9 copy.30
  192.2 29.5 %all_to_all.37 = bf16[256,5,1,128]{3,1,2,0:T(8,128)(2,1)S(1)} all-to-all(bf16[256,5,1,128]{3,1,2,0:T(8,128)(2,1)S(1)} %copy.30), channel_id=1, replica_groups=mesh['ch'=64,'sp'=4] {'ch'}, dimensions={0} | all-to-all | bytes 655360 | tf_op jit(solution)/shard_map/all_to_all | solution.py:52
  221.8 0.8 copy.32
  (5 shorter events, 0.1 us)
Async XLA Ops:
  6.5 176.2 %all-gather.2.cloned.1.call-start = ((), (), s32[]{:S(2)}) async-start(), calls=%async_computation.2 | async-start | bytes 4259840 | tf_op jit(solution)/shard_map/all_gather | solution.py:47
  9.2 42.0 %copy-start.1 = (u32[256]{0:T(256)S(1)}, u32[256]{0:T(256)}, u32[]{:S(2)}) copy-start(u32[256]{0:T(256)} %constant.14) | copy-start | bytes 3076
  9.2 43.2 %copy-start = (bf16[4]{0:T(256)(128)(2,1)S(1)}, bf16[4]{0:T(256)(128)(2,1)}, u32[]{:S(2)}) copy-start(bf16[4]{0:T(256)(128)(2,1)} %param.5) | copy-start | bytes 28
  39.7 4.4 %collective-permute-start.1 = (bf16[256,5,1,128]{3,0,1,2:T(8,128)(2,1)S(1)}, bf16[256,5,1,128]{3,0,1,2:T(8,128)(2,1)S(1)}, u32[]{:S(2)}, u32[]{:S(2)}) collective-permute-start(bf16[256,5,1,128]{3,0,1,2:T(8,128)(2,1)S(1)} %bitcast.31), channel_id=1, source_target_pairs={{4,0},{8,4},{12,8},{16,12},{20,16},{24,20},{28,24},{32,28},{36,32}... | collective-permute-start | bytes 983048 | tf_op jit(solution)/shard_map/ppermute | solution.py:17
  41.0 4.3 %collective-permute-start = (bf16[256,5,1,128]{3,0,1,2:T(8,128)(2,1)S(1)}, bf16[256,5,1,128]{3,0,1,2:T(8,128)(2,1)S(1)}, u32[]{:S(2)}, u32[]{:S(2)}) collective-permute-start(bf16[256,5,1,128]{3,0,1,2:T(8,128)(2,1)S(1)} %bitcast.32), channel_id=1, source_target_pairs={{0,4},{4,8},{8,12},{12,16},{16,20},{20,24},{24,28},{28,32},{32,36}... | collective-permute-start | bytes 983048 | tf_op jit(solution)/shard_map/ppermute | solution.py:15
  45.4 135.3 %collective-permute-start.3 = (bf16[256,1,3,128]{3,0,1,2:T(8,128)(2,1)S(1)}, bf16[256,1,3,128]{3,0,1,2:T(8,128)(2,1)S(1)}, u32[]{:S(2)}, u32[]{:S(2)}) collective-permute-start(bf16[256,1,3,128]{3,0,1,2:T(8,128)(2,1)S(1)} %get-tuple-element.6), channel_id=1, source_target_pairs={{1,0},{2,1},{3,2},{5,4},{6,5},{7,6},{9,8},{10,9},{11,10},{13,12},{... | collective-permute-start | bytes 589832 | tf_op jit(solution)/shard_map/ppermute | solution.py:17
  47.8 132.9 %collective-permute-start.2 = (bf16[256,1,3,128]{3,0,1,2:T(8,128)(2,1)S(1)}, bf16[256,1,3,128]{3,0,1,2:T(8,128)(2,1)S(1)}, u32[]{:S(2)}, u32[]{:S(2)}) collective-permute-start(bf16[256,1,3,128]{3,0,1,2:T(8,128)(2,1)S(1)} %get-tuple-element.5), channel_id=1, source_target_pairs={{0,1},{1,2},{2,3},{4,5},{5,6},{6,7},{8,9},{9,10},{10,11},{12,13},{... | collective-permute-start | bytes 589832 | tf_op jit(solution)/shard_map/ppermute | solution.py:15
  182.7 4.3 %copy-start.2 = (pred[8,17]{0,1:T(8,128)(4,1)S(1)}, pred[8,17]{0,1:T(8,128)(4,1)}, u32[]{:S(2)}) copy-start(pred[8,17]{0,1:T(8,128)(4,1)} %constant.11) | copy-start | bytes 412
Sparse Core Ops, SparseCore 0:
  10.1 82.1 all-gather.1
where the time goes:
time: 231 us; the launch traced here: 229 us
  blocking collectives  188 us (81%)
  between operations  14.2 us (6%)
  local copies, waits for them, and re-layouts  12.1 us (5%)
  starting transfers between devices  10.2 us (4%)
  matrix products  2.7 us (1%)
    unnamed x1, blocking collectives  128 us
    all_to_all x1, blocking collectives, shards(): lax.all_to_all(volume, 'ch', split_axis=2, concat_axis=0, tiled=True)  30.3 us
    all_to_all x1, blocking collectives, shards(): return lax.all_to_all(result, 'ch', split_axis=0, concat_axis=2, tiled=True)  29.5 us
    ppermute x2, starting transfers between devices, extended(): lax.ppermute(tail, axis, [(i, (i + 1) % count) for i in range(ends)])  6.44 us
    unnamed x12, local copies, waits for them, and re-layouts  4.65 us
  transfers between devices with their start and end apart: 5, of which 1 were waited for; matrix products, arithmetic and copies ran while one was open for 2% of the time, Pallas kernels for 0%

commit v1 on v0

v1 whole, which is shorter than its diff:
```python
import functools

import jax
import jax.numpy as jnp
from jax import lax
from jax.experimental import pallas as pl
from jax.experimental.pallas import tpu as pltpu
from jax.sharding import PartitionSpec as P

NYT = 4
NXT = 4
MESH = pl.DeviceIdType.MESH
F32 = jnp.float32
BF16 = jnp.bfloat16


def tap_slot(t):
    return t // 7 * 8 + t % 7 if t <= 20 else 24 + t - 20


def kernel(
    nz, v, w, b, out,
    fe, ed, rz, re, f, ge, g2, xz, X, ws, wz, wf, wt, O, oy, fo, oz,
    s_vz, r_vz, s_ed, r_ed, s_wz, r_wz, s_wy, r_wy, s_wx, r_wx,
    s_xy, r_xy, s_cc, r_cc, s_xh, r_xh, s_xf, r_xf, s_oy, r_oy, s_oz, r_oz, loc,
):
    blk = 4 * nz
    half = NYT * blk
    ch = lax.axis_index("ch")
    x = lax.axis_index("sp")
    c = lax.rem(ch, 2)
    y = lax.rem(lax.div(ch, 2), NYT)
    z = lax.div(ch, 2 * NYT)

    def at(zz, yy, cc, xx):
        return {"ch": (zz * NYT + yy) * 2 + cc, "sp": xx}

    def zk(k):
        return lax.rem(z + k + nz, nz)

    def yk(k):
        return lax.rem(y + k + NYT, NYT)

    xl, xr = lax.rem(x + NXT - 1, NXT), lax.rem(x + 1, NXT)
    sib = at(z, y, 1 - c, x)

    def send(src, dst, ss, rs, to):
        cp = pltpu.make_async_remote_copy(
            src_ref=src, dst_ref=dst, send_sem=ss, recv_sem=rs, device_id=to, device_id_type=MESH
        )
        cp.start()
        return cp

    def recv(dst, sem):
        pltpu.make_async_copy(dst, dst, sem).wait()

    def local(src, dst, sem):
        cp = pltpu.make_async_copy(src, dst, sem)
        cp.start()
        return cp

    sent = []

    bar = pltpu.get_barrier_semaphore()
    peers = [at(zk(k), y, c, x) for k in range(1, nz)]
    peers += [at(z, yk(k), c, x) for k in range(1, NYT)]
    peers += [sib, at(z, y, c, xl), at(z, y, c, xr)]
    for p in peers:
        pl.semaphore_signal(bar, inc=1, device_id=p, device_id_type=MESH)

    start = jnp.minimum(7 * x, 20)
    for i in range(7):
        ws[i] = w[start + i]
    bb = jnp.broadcast_to(b[...].astype(F32), (4, 4))
    eye = lax.broadcasted_iota(jnp.int32, (4, 4), 0) == lax.broadcasted_iota(jnp.int32, (4, 4), 1)
    col = jnp.sum(jnp.where(eye, bb, 0.0), axis=1, keepdims=True)
    ws[7] = jnp.broadcast_to(col, ws.shape[1:]).astype(BF16)

    for j in range(4):
        for p in range(5):
            base = (j * 5 + p) * nz * 8
            for k in range(nz):
                fe[base + 8 * k:base + 8 * k + 8, :] = v[j, p, k].astype(F32)
    zero_edge = jnp.zeros((20, 128), BF16)
    ed[0, 0] = zero_edge
    ed[nz - 1, 1] = zero_edge
    for k in range(1, nz):
        ed[k, 0] = fe[pl.ds(8 * k - 1, 20, stride=8 * nz), :].astype(BF16)
        ed[k - 1, 1] = fe[pl.ds(8 * k, 20, stride=8 * nz), :].astype(BF16)

    @pl.when(x == 0)
    def _():
        X[:, 0] = jnp.zeros_like(X[:, 0])

    @pl.when(x == NXT - 1)
    def _():
        X[:, 6] = jnp.zeros_like(X[:, 6])

    pl.semaphore_wait(bar, len(peers))

    for k in range(1, nz):
        sent.append(send(ws, wz.at[z], s_wz.at[k], r_wz.at[k], at(zk(k), y, c, x)))
    for k in range(1, nz):
        d = zk(k)
        sent.append(send(v.at[:, :, d], rz.at[z], s_vz.at[k], r_vz.at[k], at(d, y, c, x)))
        sent.append(send(ed.at[d], re.at[z], s_ed.at[k], r_ed.at[k], at(d, y, c, x)))
    own = [
        local(ws, wz.at[z], loc.at[0]),
        local(v.at[:, :, z], rz.at[z], loc.at[1]),
        local(ed.at[z], re.at[z], loc.at[2]),
    ]

    n_in = 2 * half
    i = lax.broadcasted_iota(jnp.int32, (n_in, n_in), 0)
    o = lax.broadcasted_iota(jnp.int32, (n_in, n_in), 1)
    to = ((i >> 2) & 1) * half + ((i >> 3) & 3) * blk + (i >> 5) * 4 + (i & 3)
    perm = jnp.where(to == o, 1.0, 0.0).astype(BF16)

    own[0].wait()
    for k in range(1, nz):
        recv(wz.at[zk(-k)], r_wz.at[k])
    for t in range(8):
        for s in range(nz):
            wf[t, 4 * s:4 * s + 4, :] = wz[s, t].astype(F32)
    yoff = pl.multiple_of(y * blk, blk)
    for t in range(8):
        wt[8 * x + t, pl.ds(yoff, blk), :] = jnp.dot(
            wf[t].astype(BF16), perm, preferred_element_type=F32
        ).astype(BF16)
    mine = wt.at[pl.ds(8 * x, 8), pl.ds(yoff, blk), :]
    for k in range(1, NYT):
        sent.append(send(mine, mine, s_wy.at[k], r_wy.at[k], at(z, yk(k), c, x)))

    own[1].wait()
    own[2].wait()
    for k in range(1, nz):
        recv(rz.at[zk(-k)], r_vz.at[k])
        recv(re.at[zk(-k)], r_ed.at[k])
    for p in range(5):
        for s in range(nz):
            for j in range(4):
                r0 = (s * 4 + j) * 8
                f[p, r0:r0 + 8, :] = rz[s, j, p].astype(F32)
    for s in range(nz):
        for side in range(2):
            ge[s, side] = re[s, side].astype(F32)
    for side in range(2):
        for p in range(5):
            for s in range(nz):
                g2[side * 5 + p, 4 * s:4 * s + 4, :] = ge[s, side, pl.ds(p, 4, stride=5), :]
    for p in range(5):
        for r in range(8):
            xz[p, r + 1] = f[p, pl.ds(r, blk, stride=8), :].astype(BF16)
        xz[p, 0] = g2[p].astype(BF16)
        xz[p, 9] = g2[5 + p].astype(BF16)

    def x_part(yy):
        return X.at[c, pl.ds(1, 5), :, pl.ds(pl.multiple_of(yy * blk, blk), blk), :]

    for k in range(1, NYT):
        d = yk(k)
        sent.append(
            send(xz.at[:, pl.ds(2 * d, 4)], x_part(y), s_xy.at[k], r_xy.at[k], at(z, d, c, x))
        )
    own_y = local(xz.at[:, pl.ds(2 * y, 4)], x_part(y), loc.at[3])

    for k in range(1, NYT):
        d = wt.at[pl.ds(8 * x, 8), pl.ds(pl.multiple_of(yk(-k) * blk, blk), blk), :]
        recv(d, r_wy.at[k])

    def first(g):
        return wt.at[pl.ds(8 * g, 4)]

    def second(g):
        return wt.at[pl.ds(8 * g + 4, 3)]

    right, left = at(z, y, c, xr), at(z, y, c, xl)
    sent.append(send(first(x), first(x), s_wx.at[0], r_wx.at[0], right))
    sent.append(send(second(x), second(x), s_wx.at[1], r_wx.at[1], left))
    sent.append(send(second(x), second(x), s_wx.at[2], r_wx.at[2], right))
    sent.append(send(first(x), first(x), s_wx.at[3], r_wx.at[3], left))

    own_y.wait()
    for k in range(1, NYT):
        recv(x_part(yk(-k)), r_xy.at[k])

    @pl.when(x < NXT - 1)
    def _():
        send(X.at[c, 5], X.at[c, 0], s_xh.at[0], r_xh.at[0], right)

    @pl.when(x > 0)
    def _():
        send(X.at[c, 1], X.at[c, 6], s_xh.at[1], r_xh.at[1], left)

    own_planes = X.at[c, pl.ds(1, 5)]
    sent.append(send(own_planes, own_planes, s_cc.at[0], r_cc.at[0], sib))

    recv(first(xl), r_wx.at[0])
    sent.append(send(first(xl), first(xl), s_wx.at[4], r_wx.at[4], right))
    recv(second(xr), r_wx.at[1])
    sent.append(send(second(xr), second(xr), s_wx.at[5], r_wx.at[5], left))

    @pl.when(x > 0)
    def _():
        recv(X.at[c, 0], r_xh.at[0])
        send(X.at[c, 0], X.at[c, 0], s_xf.at[0], r_xf.at[0], sib)

    @pl.when(x < NXT - 1)
    def _():
        recv(X.at[c, 6], r_xh.at[1])
        send(X.at[c, 6], X.at[c, 6], s_xf.at[1], r_xf.at[1], sib)

    recv(X.at[1 - c, pl.ds(1, 5)], r_cc.at[0])

    @pl.when(x > 0)
    def _():
        recv(X.at[1 - c, 0], r_xf.at[0])

    @pl.when(x < NXT - 1)
    def _():
        recv(X.at[1 - c, 6], r_xf.at[1])

    xo = lax.rem(x + 2, NXT)
    recv(second(xl), r_wx.at[2])
    recv(first(xr), r_wx.at[3])
    recv(first(xo), r_wx.at[4])
    recv(second(xo), r_wx.at[5])

    bias = wt[8 * x + 7].astype(F32)[:, 0:1]
    lane = lax.broadcasted_iota(jnp.int32, (half, 128), 1)

    def compute(p):
        acc = None
        for a in range(3):
            for bq in range(3):
                t = 9 * a + 3 * bq
                lhs = jnp.concatenate([wt[tap_slot(t + q)] for q in range(3)], axis=0)
                rhs = jnp.concatenate(
                    [
                        jnp.concatenate([X[0, p + a, r + bq], X[1, p + a, r + bq]], axis=0)
                        for r in range(2)
                    ],
                    axis=1,
                )
                part = jnp.dot(lhs, rhs, preferred_element_type=F32)
                acc = part if acc is None else acc + part
        for r in range(2):
            cols = acc[:, 128 * r:128 * r + 128]
            low = jnp.where(lane == 0, 0.0, pltpu.roll(cols[0:half], 1, 1))
            high = jnp.where(lane == 127, 0.0, pltpu.roll(cols[2 * half:], 127, 1))
            total = low + cols[half:2 * half] + high + bias
            O[p, r] = jnp.where(total > 0, total, 0.3 * total).astype(BF16)

    def out_y(p):
        for k in range(1, NYT):
            d = yk(k)
            sent.append(
                send(
                    O.at[p, :, pl.ds(pl.multiple_of(d * blk, blk), blk), :],
                    oy.at[p, pl.ds(2 * y, 2)],
                    s_oy.at[p, k], r_oy.at[p, k], at(z, d, c, x),
                )
            )
        oy[p, pl.ds(2 * y, 2)] = O[p, :, pl.ds(yoff, blk), :]

    def out_z(p):
        for k in range(1, NYT):
            recv(oy.at[p, pl.ds(2 * yk(-k), 2)], r_oy.at[p, k])
        for r in range(8):
            fo[p, blk * r:blk * r + blk, :] = oy[p, r].astype(F32)
        for m in range(blk):
            oz[p, m // 4, m % 4] = fo[p, pl.ds(m, 8, stride=blk), :].astype(BF16)
        for k in range(1, nz):
            d = zk(k)
            sent.append(
                send(oz.at[p, d], out.at[:, p, z], s_oz.at[p, k], r_oz.at[p, k], at(d, y, c, x))
            )
        return local(oz.at[p, z], out.at[:, p, z], loc.at[4 + p])

    finals = []
    for p in range(5):
        compute(p)
        out_y(p)
        if p:
            finals.append(out_z(p - 1))
    finals.append(out_z(4))

    for cp in finals:
        cp.wait()
    for p in range(5):
        for k in range(1, nz):
            recv(out.at[:, p, zk(-k)], r_oz.at[p, k])
    for cp in sent:
        cp.wait_send()

    @pl.when(x < NXT - 1)
    def _():
        recv(X.at[c, 5], s_xh.at[0])
        recv(X.at[c, 6], s_xf.at[1])

    @pl.when(x > 0)
    def _():
        recv(X.at[c, 1], s_xh.at[1])
        recv(X.at[c, 0], s_xf.at[0])


def shards(nz, volume, weight, channel_bias):
    blk = 4 * nz
    half = NYT * blk
    n_in = 2 * half
    v = volume.reshape(4, 5, nz, 8, 128)
    w = weight.transpose(1, 0, 2)
    b = channel_bias.reshape(1, 4)
    vm = pltpu.VMEM
    dma = pltpu.SemaphoreType.DMA
    out = pl.pallas_call(
        functools.partial(kernel, nz),
        out_shape=jax.ShapeDtypeStruct((4, 5, nz, 8, 128), BF16),
        in_specs=[pl.BlockSpec(memory_space=pltpu.VMEM)] * 3,
        out_specs=pl.BlockSpec(memory_space=pltpu.VMEM),
        scratch_shapes=[
            vm((20 * 8 * nz, 128), F32),
            vm((nz, 2, 20, 128), BF16),
            vm((nz, 4, 5, 8, 128), BF16),
            vm((nz, 2, 20, 128), BF16),
            vm((5, blk * 8, 128), F32),
            vm((nz, 2, 20, 128), F32),
            vm((10, blk, 128), F32),
            vm((5, 10, blk, 128), BF16),
            vm((2, 7, 4, half, 128), BF16),
            vm((8, 4, n_in), BF16),
            vm((nz, 8, 4, n_in), BF16),
            vm((8, blk, n_in), F32),
            vm((32, half, n_in), BF16),
            vm((5, 2, half, 128), BF16),
            vm((5, 8, blk, 128), BF16),
            vm((5, 8 * blk, 128), F32),
            vm((5, nz, 4, 8, 128), BF16),
            dma((nz,)), dma((nz,)), dma((nz,)), dma((nz,)), dma((nz,)), dma((nz,)),
            dma((4,)), dma((4,)), dma((6,)), dma((6,)),
            dma((4,)), dma((4,)), dma((1,)), dma((1,)), dma((2,)), dma((2,)), dma((2,)), dma((2,)),
            dma((5, 4)), dma((5, 4)), dma((5, nz)), dma((5, nz)), dma((9,)),
        ],
        compiler_params=pltpu.CompilerParams(
            collective_id=0, has_side_effects=True, vmem_limit_bytes=40 * 1024 * 1024
        ),
        cost_estimate=pl.CostEstimate(
            flops=2 * 640 * n_in * n_in * 27, bytes_accessed=2 * v.size * 2, transcendentals=0
        ),
    )(v, w, b)
    return out.reshape(volume.shape)


def solution(mesh):
    nz = mesh.shape["ch"] // (2 * NYT)
    return jax.shard_map(
        functools.partial(shards, nz),
        mesh=mesh,
        in_specs=(P("ch", "sp", None, None), P("ch", None, None), P("ch")),
        out_specs=P("ch", "sp", None, None),
        check_vma=False,
    )
```

time: 231 us -> 66.8 us (0.29)
  blocking collectives: 188 us -> 0 us
  Pallas kernels: 0 us -> 62.7 us
  between operations: 14.2 us -> 0.01 us
  starting transfers between devices: 10.2 us -> 0 us
  local copies, waits for them, and re-layouts: 12.1 us -> 3.17 us
  matrix products: 2.7 us -> 0 us
    unnamed x1 -> x0, blocking collectives: 128 us -> none
    pallas_call x0 -> x1, Pallas kernels: none -> 62.7 us  [shards(): pl.pallas_call(functools.partial(kernel, nz), out_shape=jax.ShapeDtypeStr...]
    all_to_all x2 -> x0, blocking collectives: 59.8 us -> none  [the longest x1 30.3 us: shards(): lax.all_to_all(volume, 'ch', split_axis=2, concat_axis=0, tiled=True)]
    ppermute x4 -> x0, starting transfers between devices: 10.2 us -> none  [the longest x2 6.44 us: extended(): lax.ppermute(tail, axis, [(i, (i + 1) % count) for i in range(ends)])]
    all_gather x1 -> x0, local copies, waits for them, and re-layouts: 4.25 us -> none  [shards(): lax.all_gather(weight, 'ch', axis=0, tiled=True)]
    conv_general_dilated x1 -> x0, matrix products: 2.7 us -> none  [convolve(): lax.conv_general_dilated(portion[None], kernel, (1, 1, 1), edge_pad, dime...]
    unnamed x12 -> x7, local copies, waits for them, and re-layouts: 4.65 us -> 3.17 us
  transfers between devices with their start and end apart: 5 -> 0, of which waited for: 1 -> 0; matrix products, arithmetic and copies ran while one was open for 2% -> 0% of each run, Pallas kernels for 0% -> 0%
where the time goes in v1:
time: 66.8 us; the launch traced here: 65.9 us
  Pallas kernels  62.7 us (94%)
  local copies, waits for them, and re-layouts  3.17 us (5%)
    pallas_call x1, Pallas kernels, shards(): pl.pallas_call(functools.partial(kernel, nz), out_shape=jax.ShapeDtypeStr...  62.7 us
    unnamed x7, local copies, waits for them, and re-layouts  3.17 us

profile of v1, /device:TPU:2, one launch (start us, length us, event | category | flops | bytes accessed | tf_op | source)
XLA Modules:
  0.0 65.9 jit_solution(15453796449487449736)
XLA Ops:
  0.0 0.0 copy-start.2
  0.0 0.7 copy-done.2
  0.7 0.0 copy-start
  0.7 1.0 %copy-done = bf16[4,5,64,128]{3,2,1,0:T(8,128)(2,1)S(1)} copy-done((bf16[4,5,64,128]{3,2,1,0:T(8,128)(2,1)S(1)}, bf16[4,5,64,128]{3,2,1,0:T(8,128)(2,1)}, u32[]{:S(2)}) %copy-start) | copy-done | bytes 327704
  1.6 0.0 copy-start.1
  1.6 0.8 %copy-done.1 = bf16[4,27,256]{2,0,1:T(4,128)(2,1)S(1)} copy-done((bf16[4,27,256]{2,0,1:T(4,128)(2,1)S(1)}, bf16[4,27,256]{2,0,1:T(4,128)(2,1)}, u32[]{:S(2)}) %copy-start.1) | copy-done | bytes 55320
  2.4 62.7 %shard_map.37 = bf16[4,5,8,8,128]{4,3,2,1,0:T(8,128)(2,1)S(1)} custom-call(bf16[4,5,8,8,128]{4,3,2,1,0:T(8,128)(2,1)S(1)} %bitcast.5, bf16[27,4,256]{2,1,0:T(4,128)(2,1)S(1)} %bitcast.6, bf16[1,4]{1,0:T(2,128)(2,1)S(1)} %bitcast.7), custom_call_target="tpu_custom_call" | custom-call | flops 2264924160 | bytes 655360 | tf_op jit(solution)/shard_map/pallas_call | solution.py:316
  65.2 0.7 %copy.5 = bf16[4,5,64,128]{3,2,1,0:T(8,128)(2,1)} copy(bf16[4,5,64,128]{3,2,1,0:T(8,128)(2,1)S(1)} %bitcast.4) | data formatting | bytes 655360
Async XLA Ops:
  0.0 0.7 copy-start.2
  0.7 1.0 %copy-start = (bf16[4,5,64,128]{3,2,1,0:T(8,128)(2,1)S(1)}, bf16[4,5,64,128]{3,2,1,0:T(8,128)(2,1)}, u32[]{:S(2)}) copy-start(bf16[4,5,64,128]{3,2,1,0:T(8,128)(2,1)} %param.3) | copy-start | bytes 983044
  1.6 0.8 %copy-start.1 = (bf16[4,27,256]{2,0,1:T(4,128)(2,1)S(1)}, bf16[4,27,256]{2,0,1:T(4,128)(2,1)}, u32[]{:S(2)}) copy-start(bf16[4,27,256]{2,0,1:T(4,128)(2,1)} %param.4) | copy-start | bytes 165892

commit v2 on v1

--- a/solution.py
+++ b/solution.py
@@ -9,6 +9,8 @@
 
 NYT = 4
 NXT = 4
+PLANES = (4, 0, 1, 2, 3)
+OUT_LAG = 2
 MESH = pl.DeviceIdType.MESH
 F32 = jnp.float32
 BF16 = jnp.bfloat16
@@ -19,10 +21,10 @@
 
 
 def kernel(
-    nz, v, w, b, out,
-    fe, ed, rz, re, f, ge, g2, xz, X, ws, wz, wf, wt, O, oy, fo, oz,
+    nz, v_hbm, w_hbm, b_hbm, out,
+    v, b, fe, ed, rz, re, f, ge, g2, xz, X, ws, wz, wf, wt, O, oy, fo, oz,
     s_vz, r_vz, s_ed, r_ed, s_wz, r_wz, s_wy, r_wy, s_wx, r_wx,
-    s_xy, r_xy, s_cc, r_cc, s_xh, r_xh, s_xf, r_xf, s_oy, r_oy, s_oz, r_oz, loc,
+    s_xy, r_xy, s_cc, r_cc, s_xh, r_xh, s_xf, r_xf, s_oy, r_oy, s_oz, r_oz, loc, loc_p,
 ):
     blk = 4 * nz
     half = NYT * blk
@@ -43,6 +45,7 @@
 
     xl, xr = lax.rem(x + NXT - 1, NXT), lax.rem(x + 1, NXT)
     sib = at(z, y, 1 - c, x)
+    right, left = at(z, y, c, xr), at(z, y, c, xl)
 
     def send(src, dst, ss, rs, to):
         cp = pltpu.make_async_remote_copy(
@@ -60,22 +63,42 @@
         return cp
 
     sent = []
+    z_order = sorted(range(1, nz), key=lambda k: -min(k, nz - k))
 
     bar = pltpu.get_barrier_semaphore()
     peers = [at(zk(k), y, c, x) for k in range(1, nz)]
     peers += [at(z, yk(k), c, x) for k in range(1, NYT)]
-    peers += [sib, at(z, y, c, xl), at(z, y, c, xr)]
+    peers += [sib, left, right]
+    start = jnp.minimum(7 * x, 20)
+    loads = [
+        local(v_hbm, v, loc.at[0]),
+        local(b_hbm, b, loc.at[1]),
+        local(w_hbm.at[pl.ds(start, 7)], ws.at[pl.ds(0, 7)], loc.at[2]),
+    ]
     for p in peers:
         pl.semaphore_signal(bar, inc=1, device_id=p, device_id_type=MESH)
 
-    start = jnp.minimum(7 * x, 20)
-    for i in range(7):
-        ws[i] = w[start + i]
+    @pl.when(x == 0)
+    def _():
+        X[:, 0] = jnp.zeros_like(X[:, 0])
+
+    @pl.when(x == NXT - 1)
+    def _():
+        X[:, 6] = jnp.zeros_like(X[:, 6])
+
+    n_in = 2 * half
+    i = lax.broadcasted_iota(jnp.int32, (n_in, n_in), 0)
+    o = lax.broadcasted_iota(jnp.int32, (n_in, n_in), 1)
+    to = ((i >> 2) & 1) * half + ((i >> 3) & 3) * blk + (i >> 5) * 4 + (i & 3)
+    perm = jnp.where(to == o, 1.0, 0.0).astype(BF16)
+
+    loads[1].wait()
     bb = jnp.broadcast_to(b[...].astype(F32), (4, 4))
     eye = lax.broadcasted_iota(jnp.int32, (4, 4), 0) == lax.broadcasted_iota(jnp.int32, (4, 4), 1)
     col = jnp.sum(jnp.where(eye, bb, 0.0), axis=1, keepdims=True)
     ws[7] = jnp.broadcast_to(col, ws.shape[1:]).astype(BF16)
 
+    loads[0].wait()
     for j in range(4):
         for p in range(5):
             base = (j * 5 + p) * nz * 8
@@ -87,37 +110,28 @@
     for k in range(1, nz):
         ed[k, 0] = fe[pl.ds(8 * k - 1, 20, stride=8 * nz), :].astype(BF16)
         ed[k - 1, 1] = fe[pl.ds(8 * k, 20, stride=8 * nz), :].astype(BF16)
-
-    @pl.when(x == 0)
-    def _():
-        X[:, 0] = jnp.zeros_like(X[:, 0])
-
-    @pl.when(x == NXT - 1)
-    def _():
-        X[:, 6] = jnp.zeros_like(X[:, 6])
+    loads[2].wait()
 
     pl.semaphore_wait(bar, len(peers))
 
-    for k in range(1, nz):
+    for k in z_order:
         sent.append(send(ws, wz.at[z], s_wz.at[k], r_wz.at[k], at(zk(k), y, c, x)))
-    for k in range(1, nz):
+    own_w = local(ws, wz.at[z], loc.at[3])
+    for k in z_order:
         d = zk(k)
-        sent.append(send(v.at[:, :, d], rz.at[z], s_vz.at[k], r_vz.at[k], at(d, y, c, x)))
         sent.append(send(ed.at[d], re.at[z], s_ed.at[k], r_ed.at[k], at(d, y, c, x)))
-    own = [
-        local(ws, wz.at[z], loc.at[0]),
-        local(v.at[:, :, z], rz.at[z], loc.at[1]),
-        local(ed.at[z], re.at[z], loc.at[2]),
-    ]
-
-    n_in = 2 * half
-    i = lax.broadcasted_iota(jnp.int32, (n_in, n_in), 0)
-    o = lax.broadcasted_iota(jnp.int32, (n_in, n_in), 1)
-    to = ((i >> 2) & 1) * half + ((i >> 3) & 3) * blk + (i >> 5) * 4 + (i & 3)
-    perm = jnp.where(to == o, 1.0, 0.0).astype(BF16)
-
-    own[0].wait()
-    for k in range(1, nz):
+    own_e = local(ed.at[z], re.at[z], loc.at[4])
+    own_v = {}
+    for p in PLANES:
+        for k in z_order:
+            d = zk(k)
+            sent.append(
+                send(v.at[:, p, d], rz.at[p, z], s_vz.at[p, k], r_vz.at[p, k], at(d, y, c, x))
+            )
+        own_v[p] = local(v.at[:, p, z], rz.at[p, z], loc_p.at[p])
+
+    own_w.wait()
+    for k in z_order[::-1]:
         recv(wz.at[zk(-k)], r_wz.at[k])
     for t in range(8):
         for s in range(nz):
@@ -127,20 +141,43 @@
         wt[8 * x + t, pl.ds(yoff, blk), :] = jnp.dot(
             wf[t].astype(BF16), perm, preferred_element_type=F32
         ).astype(BF16)
-    mine = wt.at[pl.ds(8 * x, 8), pl.ds(yoff, blk), :]
-    for k in range(1, NYT):
-        sent.append(send(mine, mine, s_wy.at[k], r_wy.at[k], at(z, yk(k), c, x)))
-
-    own[1].wait()
-    own[2].wait()
-    for k in range(1, nz):
-        recv(rz.at[zk(-k)], r_vz.at[k])
-        recv(re.at[zk(-k)], r_ed.at[k])
-    for p in range(5):
+
+    def w_part(h, yy):
+        return wt.at[pl.ds(8 * x + 4 * h, 4), pl.ds(pl.multiple_of(yy * blk, blk), blk), :]
+
+    for h in range(2):
+        for k in (2, 1, 3):
+            mine = w_part(h, y)
+            sent.append(send(mine, mine, s_wy.at[h, k], r_wy.at[h, k], at(z, yk(k), c, x)))
+
+    def x_part(p, yy):
+        return X.at[c, p + 1, :, pl.ds(pl.multiple_of(yy * blk, blk), blk), :]
+
+    own_y = {}
+
+    def volume_y(p):
+        own_v[p].wait()
+        for k in z_order[::-1]:
+            recv(rz.at[p, zk(-k)], r_vz.at[p, k])
         for s in range(nz):
             for j in range(4):
                 r0 = (s * 4 + j) * 8
-                f[p, r0:r0 + 8, :] = rz[s, j, p].astype(F32)
+                f[p, r0:r0 + 8, :] = rz[p, s, j].astype(F32)
+        for r in range(8):
+            xz[p, r + 1] = f[p, pl.ds(r, blk, stride=8), :].astype(BF16)
+        for k in (2, 1, 3):
+            d = yk(k)
+            sent.append(
+                send(
+                    xz.at[p, pl.ds(2 * d, 4)], x_part(p, y), s_xy.at[p, k], r_xy.at[p, k],
+                    at(z, d, c, x),
+                )
+            )
+        own_y[p] = local(xz.at[p, pl.ds(2 * y, 4)], x_part(p, y), loc_p.at[5 + p])
+
+    own_e.wait()
+    for k in z_order[::-1]:
+        recv(re.at[zk(-k)], r_ed.at[k])
     for s in range(nz):
         for side in range(2):
             ge[s, side] = re[s, side].astype(F32)
@@ -148,25 +185,10 @@
         for p in range(5):
             for s in range(nz):
                 g2[side * 5 + p, 4 * s:4 * s + 4, :] = ge[s, side, pl.ds(p, 4, stride=5), :]
-    for p in range(5):
-        for r in range(8):
-            xz[p, r + 1] = f[p, pl.ds(r, blk, stride=8), :].astype(BF16)
-        xz[p, 0] = g2[p].astype(BF16)
-        xz[p, 9] = g2[5 + p].astype(BF16)
-
-    def x_part(yy):
-        return X.at[c, pl.ds(1, 5), :, pl.ds(pl.multiple_of(yy * blk, blk), blk), :]
-
-    for k in range(1, NYT):
-        d = yk(k)
-        sent.append(
-            send(xz.at[:, pl.ds(2 * d, 4)], x_part(y), s_xy.at[k], r_xy.at[k], at(z, d, c, x))
-        )
-    own_y = local(xz.at[:, pl.ds(2 * y, 4)], x_part(y), loc.at[3])
-
-    for k in range(1, NYT):
-        d = wt.at[pl.ds(8 * x, 8), pl.ds(pl.multiple_of(yk(-k) * blk, blk), blk), :]
-        recv(d, r_wy.at[k])
+            xz[p, 9 * side] = g2[side * 5 + p].astype(BF16)
+
+    for p in PLANES[:3]:
+        volume_y(p)
 
     def first(g):
         return wt.at[pl.ds(8 * g, 4)]
@@ -174,26 +196,31 @@
     def second(g):
         return wt.at[pl.ds(8 * g + 4, 3)]
 
-    right, left = at(z, y, c, xr), at(z, y, c, xl)
+    for k in range(1, NYT):
+        recv(w_part(0, yk(-k)), r_wy.at[0, k])
     sent.append(send(first(x), first(x), s_wx.at[0], r_wx.at[0], right))
+    for k in range(1, NYT):
+        recv(w_part(1, yk(-k)), r_wy.at[1, k])
     sent.append(send(second(x), second(x), s_wx.at[1], r_wx.at[1], left))
     sent.append(send(second(x), second(x), s_wx.at[2], r_wx.at[2], right))
     sent.append(send(first(x), first(x), s_wx.at[3], r_wx.at[3], left))
 
-    own_y.wait()
-    for k in range(1, NYT):
-        recv(x_part(yk(-k)), r_xy.at[k])
-
-    @pl.when(x < NXT - 1)
-    def _():
-        send(X.at[c, 5], X.at[c, 0], s_xh.at[0], r_xh.at[0], right)
-
-    @pl.when(x > 0)
-    def _():
-        send(X.at[c, 1], X.at[c, 6], s_xh.at[1], r_xh.at[1], left)
-
-    own_planes = X.at[c, pl.ds(1, 5)]
-    sent.append(send(own_planes, own_planes, s_cc.at[0], r_cc.at[0], sib))
+    for p in PLANES[3:]:
+        volume_y(p)
+
+    for p in PLANES:
+        own_y[p].wait()
+        for k in range(1, NYT):
+            recv(x_part(p, yk(-k)), r_xy.at[p, k])
+        if p == 4:
+            @pl.when(x < NXT - 1)
+            def _():
+                send(X.at[c, 5], X.at[c, 0], s_xh.at[0], r_xh.at[0], right)
+        if p == 0:
+            @pl.when(x > 0)
+            def _():
+                send(X.at[c, 1], X.at[c, 6], s_xh.at[1], r_xh.at[1], left)
+        sent.append(send(X.at[c, p + 1], X.at[c, p + 1], s_cc.at[p], r_cc.at[p], sib))
 
     recv(first(xl), r_wx.at[0])
     sent.append(send(first(xl), first(xl), s_wx.at[4], r_wx.at[4], right))
@@ -210,7 +237,8 @@
         recv(X.at[c, 6], r_xh.at[1])
         send(X.at[c, 6], X.at[c, 6], s_xf.at[1], r_xf.at[1], sib)
 
-    recv(X.at[1 - c, pl.ds(1, 5)], r_cc.at[0])
+    for p in PLANES:
+        recv(X.at[1 - c, p + 1], r_cc.at[p])
 
     @pl.when(x > 0)
     def _():
@@ -252,7 +280,7 @@
             O[p, r] = jnp.where(total > 0, total, 0.3 * total).astype(BF16)
 
     def out_y(p):
-        for k in range(1, NYT):
+        for k in (2, 1, 3):
             d = yk(k)
             sent.append(
                 send(
@@ -270,24 +298,26 @@
             fo[p, blk * r:blk * r + blk, :] = oy[p, r].astype(F32)
         for m in range(blk):
             oz[p, m // 4, m % 4] = fo[p, pl.ds(m, 8, stride=blk), :].astype(BF16)
-        for k in range(1, nz):
+        for k in z_order:
             d = zk(k)
             sent.append(
                 send(oz.at[p, d], out.at[:, p, z], s_oz.at[p, k], r_oz.at[p, k], at(d, y, c, x))
             )
-        return local(oz.at[p, z], out.at[:, p, z], loc.at[4 + p])
+        return local(oz.at[p, z], out.at[:, p, z], loc_p.at[10 + p])
 
     finals = []
-    for p in range(5):
+    order = [1, 2, 3, 0, 4]
+    for n, p in enumerate(order):
         compute(p)
         out_y(p)
-        if p:
-            finals.append(out_z(p - 1))
-    finals.append(out_z(4))
+        if n >= OUT_LAG:
+            finals.append(out_z(order[n - OUT_LAG]))
+    for p in order[5 - OUT_LAG:]:
+        finals.append(out_z(p))
 
     for cp in finals:
         cp.wait()
-    for p in range(5):
+    for p in order:
         for k in range(1, nz):
             recv(out.at[:, p, zk(-k)], r_oz.at[p, k])
     for cp in sent:
@@ -316,12 +346,14 @@
     out = pl.pallas_call(
         functools.partial(kernel, nz),
         out_shape=jax.ShapeDtypeStruct((4, 5, nz, 8, 128), BF16),
-        in_specs=[pl.BlockSpec(memory_space=pltpu.VMEM)] * 3,
+        in_specs=[pl.BlockSpec(memory_space=pl.ANY)] * 3,
         out_specs=pl.BlockSpec(memory_space=pltpu.VMEM),
         scratch_shapes=[
+            vm((4, 5, nz, 8, 128), BF16),
+            vm((1, 4), BF16),
             vm((20 * 8 * nz, 128), F32),
             vm((nz, 2, 20, 128), BF16),
-            vm((nz, 4, 5, 8, 128), BF16),
+            vm((5, nz, 4, 8, 128), BF16),
             vm((nz, 2, 20, 128), BF16),
             vm((5, blk * 8, 128), F32),
             vm((nz, 2, 20, 128), F32),
@@ -336,13 +368,13 @@
             vm((5, 8, blk, 128), BF16),
             vm((5, 8 * blk, 128), F32),
             vm((5, nz, 4, 8, 128), BF16),
-            dma((nz,)), dma((nz,)), dma((nz,)), dma((nz,)), dma((nz,)), dma((nz,)),
-            dma((4,)), dma((4,)), dma((6,)), dma((6,)),
-            dma((4,)), dma((4,)), dma((1,)), dma((1,)), dma((2,)), dma((2,)), dma((2,)), dma((2,)),
-            dma((5, 4)), dma((5, 4)), dma((5, nz)), dma((5, nz)), dma((9,)),
+            dma((5, nz)), dma((5, nz)), dma((nz,)), dma((nz,)), dma((nz,)), dma((nz,)),
+            dma((2, 4)), dma((2, 4)), dma((6,)), dma((6,)),
+            dma((5, 4)), dma((5, 4)), dma((5,)), dma((5,)), dma((2,)), dma((2,)), dma((2,)), dma((2,)),
+            dma((5, 4)), dma((5, 4)), dma((5, nz)), dma((5, nz)), dma((5,)), dma((15,)),
         ],
         compiler_params=pltpu.CompilerParams(
-            collective_id=0, has_side_effects=True, vmem_limit_bytes=40 * 1024 * 1024
+            collective_id=0, has_side_effects=True, vmem_limit_bytes=63 * 1024 * 1024
         ),
         cost_estimate=pl.CostEstimate(
             flops=2 * 640 * n_in * n_in * 27, bytes_accessed=2 * v.size * 2, transcendentals=0

time: 66.8 us -> 59.4 us (0.89)
  Pallas kernels: 62.7 us -> 56.9 us
  local copies, waits for them, and re-layouts: 3.17 us -> 1.72 us
    pallas_call x1, Pallas kernels: 62.7 us -> 56.9 us  [shards(): pl.pallas_call(functools.partial(kernel, nz), out_shape=jax.ShapeDtypeStr...]
    unnamed x7 -> x1, local copies, waits for them, and re-layouts: 3.17 us -> 1.72 us
where the time goes in v2:
time: 59.4 us; the launch traced here: 58.6 us
  Pallas kernels  56.9 us (96%)
  local copies, waits for them, and re-layouts  1.72 us (3%)
    pallas_call x1, Pallas kernels, shards(): pl.pallas_call(functools.partial(kernel, nz), out_shape=jax.ShapeDtypeStr...  56.9 us
    unnamed x1, local copies, waits for them, and re-layouts  1.72 us

profile of v2, /device:TPU:2, one launch (start us, length us, event | category | flops | bytes accessed | tf_op | source)
XLA Modules:
  0.0 58.6 jit_solution(11245450856542161189)
XLA Ops:
  0.0 56.9 %shard_map.37 = bf16[4,5,8,8,128]{4,3,2,1,0:T(8,128)(2,1)} custom-call(bf16[4,5,8,8,128]{4,3,2,1,0:T(8,128)(2,1)} %bitcast.5, bf16[27,4,256]{2,1,0:T(4,128)(2,1)} %bitcast.6, bf16[1,4]{1,0:T(2,128)(2,1)} %bitcast.7), custom_call_target="tpu_custom_call" | custom-call | flops 2264924160 | bytes 655360 | tf_op jit(solution)/shard_map/pallas_call | solution.py:346
  56.9 1.7 %copy.5 = bf16[4,5,64,128]{3,2,1,0:T(8,128)(2,1)} copy(bf16[4,5,64,128]{3,2,1,0:T(8,128)(2,1)} %bitcast.4) | data formatting | bytes 655360

commit v3 on v2

--- a/solution.py
+++ b/solution.py
@@ -10,20 +10,22 @@
 NYT = 4
 NXT = 4
 PLANES = (4, 0, 1, 2, 3)
-OUT_LAG = 2
+OUT_LAG = 3
+N1 = 5
+STEPS = "v4 v0 f1 f3 g0 v1 f2 v2 v3 g1 g3 c4 c0 g2 c1 c2 c3 h".split()
 MESH = pl.DeviceIdType.MESH
 F32 = jnp.float32
 BF16 = jnp.bfloat16
 
 
 def tap_slot(t):
-    return t // 7 * 8 + t % 7 if t <= 20 else 24 + t - 20
+    return (t // 7, t % 7) if t <= 20 else (3, t - 20)
 
 
 def kernel(
     nz, v_hbm, w_hbm, b_hbm, out,
     v, b, fe, ed, rz, re, f, ge, g2, xz, X, ws, wz, wf, wt, O, oy, fo, oz,
-    s_vz, r_vz, s_ed, r_ed, s_wz, r_wz, s_wy, r_wy, s_wx, r_wx,
+    s_vz, r_vz, s_ed, r_ed, s_wz, r_wz, s_wa, r_wa, s_wb, r_wb,
     s_xy, r_xy, s_cc, r_cc, s_xh, r_xh, s_xf, r_xf, s_oy, r_oy, s_oz, r_oz, loc, loc_p,
 ):
     blk = 4 * nz
@@ -68,7 +70,8 @@
     bar = pltpu.get_barrier_semaphore()
     peers = [at(zk(k), y, c, x) for k in range(1, nz)]
     peers += [at(z, yk(k), c, x) for k in range(1, NYT)]
-    peers += [sib, left, right]
+    peers += [at(z, y, c, lax.rem(x + k, NXT)) for k in range(1, NXT)]
+    peers += [sib]
     start = jnp.minimum(7 * x, 20)
     loads = [
         local(v_hbm, v, loc.at[0]),
@@ -138,17 +141,64 @@
             wf[t, 4 * s:4 * s + 4, :] = wz[s, t].astype(F32)
     yoff = pl.multiple_of(y * blk, blk)
     for t in range(8):
-        wt[8 * x + t, pl.ds(yoff, blk), :] = jnp.dot(
+        wt[x, t, pl.ds(yoff, blk), :] = jnp.dot(
             wf[t].astype(BF16), perm, preferred_element_type=F32
         ).astype(BF16)
 
-    def w_part(h, yy):
-        return wt.at[pl.ds(8 * x + 4 * h, 4), pl.ds(pl.multiple_of(yy * blk, blk), blk), :]
-
-    for h in range(2):
-        for k in (2, 1, 3):
-            mine = w_part(h, y)
-            sent.append(send(mine, mine, s_wy.at[h, k], r_wy.at[h, k], at(z, yk(k), c, x)))
+    def rows(yy):
+        return pl.ds(pl.multiple_of(yy * blk, blk), blk)
+
+    def part_rows(yy, h):
+        if h is None:
+            return rows(yy)
+        return pl.ds(pl.multiple_of(yy * blk + h * (blk // 2), blk // 2), blk // 2)
+
+    def w1(g, yy, h=None):
+        return wt.at[g, pl.ds(0, N1), part_rows(yy, h), :]
+
+    def w2(g, yy, h=None):
+        return wt.at[g, pl.ds(N1, 7 - N1), part_rows(yy, h), :]
+
+    def w3(yy):
+        return wt.at[x, 7, rows(yy), :]
+
+    def xk(k):
+        return lax.rem(x + k + NXT, NXT)
+
+    for k in (2, 1, 3):
+        sent.append(send(w1(x, y), w1(x, y), s_wa.at[0, k], r_wa.at[0, k], at(z, yk(k), c, x)))
+        sent.append(send(w2(x, y), w2(x, y), s_wa.at[1, k], r_wa.at[1, k], at(z, y, c, xk(k))))
+        sent.append(send(w3(y), w3(y), s_wa.at[2, k], r_wa.at[2, k], at(z, yk(k), c, x)))
+
+    def forward(q):
+        yq, xq = yk(-q), xk(-q)
+        if q:
+            recv(w1(x, yq), r_wa.at[0, q])
+        for k in (1, 3):
+            to = at(z, y, c, xk(k))
+            sent.append(send(w1(x, yq), w1(x, yq), s_wb.at[0, q, k], r_wb.at[0, q, k], to))
+        if q:
+            recv(w2(xq, y), r_wa.at[1, q])
+        for k in (1, 3):
+            to = at(z, yk(k), c, x)
+            sent.append(send(w2(xq, y), w2(xq, y), s_wb.at[1, q, k], r_wb.at[1, q, k], to))
+
+    def pass_on(q):
+        yq, xq = yk(-q), xk(-q)
+        recv(w1(xk(-1), yq), r_wb.at[0, q, 1])
+        half0 = w1(xk(-1), yq, 0)
+        sent.append(send(half0, half0, s_wb.at[0, q, 2], r_wb.at[0, q, 2], at(z, y, c, xk(1))))
+        recv(w1(xk(1), yq), r_wb.at[0, q, 3])
+        half1 = w1(xk(1), yq, 1)
+        sent.append(send(half1, half1, s_wb.at[0, q, 0], r_wb.at[0, q, 0], at(z, y, c, xk(-1))))
+        recv(w2(xq, yk(-1)), r_wb.at[1, q, 1])
+        half2 = w2(xq, yk(-1), 0)
+        sent.append(send(half2, half2, s_wb.at[1, q, 2], r_wb.at[1, q, 2], at(z, yk(1), c, x)))
+        recv(w2(xq, yk(1)), r_wb.at[1, q, 3])
+        half3 = w2(xq, yk(1), 1)
+        sent.append(send(half3, half3, s_wb.at[1, q, 0], r_wb.at[1, q, 0], at(z, yk(-1), c, x)))
+
+    forward(0)
 
     def x_part(p, yy):
         return X.at[c, p + 1, :, pl.ds(pl.multiple_of(yy * blk, blk), blk), :]
@@ -187,28 +237,7 @@
                 g2[side * 5 + p, 4 * s:4 * s + 4, :] = ge[s, side, pl.ds(p, 4, stride=5), :]
             xz[p, 9 * side] = g2[side * 5 + p].astype(BF16)
 
-    for p in PLANES[:3]:
-        volume_y(p)
-
-    def first(g):
-        return wt.at[pl.ds(8 * g, 4)]
-
-    def second(g):
-        return wt.at[pl.ds(8 * g + 4, 3)]
-
-    for k in range(1, NYT):
-        recv(w_part(0, yk(-k)), r_wy.at[0, k])
-    sent.append(send(first(x), first(x), s_wx.at[0], r_wx.at[0], right))
-    for k in range(1, NYT):
-        recv(w_part(1, yk(-k)), r_wy.at[1, k])
-    sent.append(send(second(x), second(x), s_wx.at[1], r_wx.at[1], left))
-    sent.append(send(second(x), second(x), s_wx.at[2], r_wx.at[2], right))
-    sent.append(send(first(x), first(x), s_wx.at[3], r_wx.at[3], left))
-
-    for p in PLANES[3:]:
-        volume_y(p)
-
-    for p in PLANES:
+    def share(p):
         own_y[p].wait()
         for k in range(1, NYT):
             recv(x_part(p, yk(-k)), r_xy.at[p, k])
@@ -222,39 +251,49 @@
                 send(X.at[c, 1], X.at[c, 6], s_xh.at[1], r_xh.at[1], left)
         sent.append(send(X.at[c, p + 1], X.at[c, p + 1], s_cc.at[p], r_cc.at[p], sib))
 
-    recv(first(xl), r_wx.at[0])
-    sent.append(send(first(xl), first(xl), s_wx.at[4], r_wx.at[4], right))
-    recv(second(xr), r_wx.at[1])
-    sent.append(send(second(xr), second(xr), s_wx.at[5], r_wx.at[5], left))
-
-    @pl.when(x > 0)
-    def _():
-        recv(X.at[c, 0], r_xh.at[0])
-        send(X.at[c, 0], X.at[c, 0], s_xf.at[0], r_xf.at[0], sib)
-
-    @pl.when(x < NXT - 1)
-    def _():
-        recv(X.at[c, 6], r_xh.at[1])
-        send(X.at[c, 6], X.at[c, 6], s_xf.at[1], r_xf.at[1], sib)
+    def halo():
+        @pl.when(x > 0)
+        def _():
+            recv(X.at[c, 0], r_xh.at[0])
+            send(X.at[c, 0], X.at[c, 0], s_xf.at[0], r_xf.at[0], sib)
+
+        @pl.when(x < NXT - 1)
+        def _():
+            recv(X.at[c, 6], r_xh.at[1])
+            send(X.at[c, 6], X.at[c, 6], s_xf.at[1], r_xf.at[1], sib)
+
+    for step in STEPS:
+        if step[0] == "v":
+            volume_y(int(step[1]))
+        elif step[0] == "f":
+            forward(int(step[1]))
+        elif step[0] == "g":
+            pass_on(int(step[1]))
+        elif step[0] == "c":
+            share(int(step[1]))
+        else:
+            halo()
 
     for p in PLANES:
         recv(X.at[1 - c, p + 1], r_cc.at[p])
 
-    @pl.when(x > 0)
-    def _():
-        recv(X.at[1 - c, 0], r_xf.at[0])
-
-    @pl.when(x < NXT - 1)
-    def _():
-        recv(X.at[1 - c, 6], r_xf.at[1])
-
-    xo = lax.rem(x + 2, NXT)
-    recv(second(xl), r_wx.at[2])
-    recv(first(xr), r_wx.at[3])
-    recv(first(xo), r_wx.at[4])
-    recv(second(xo), r_wx.at[5])
-
-    bias = wt[8 * x + 7].astype(F32)[:, 0:1]
+    for q in range(NXT):
+        for h, k in ((0, 2), (1, 0)):
+            recv(w1(xk(2), yk(-q), h), r_wb.at[0, q, k])
+            recv(w2(xk(-q), yk(2), h), r_wb.at[1, q, k])
+    for k in range(1, NYT):
+        recv(w3(yk(-k)), r_wa.at[2, k])
+
+    def halo_wait():
+        @pl.when(x > 0)
+        def _():
+            recv(X.at[1 - c, 0], r_xf.at[0])
+
+        @pl.when(x < NXT - 1)
+        def _():
+            recv(X.at[1 - c, 6], r_xf.at[1])
+
+    bias = wt[x, 7].astype(F32)[:, 0:1]
     lane = lax.broadcasted_iota(jnp.int32, (half, 128), 1)
 
     def compute(p):
@@ -308,6 +347,8 @@
     finals = []
     order = [1, 2, 3, 0, 4]
     for n, p in enumerate(order):
+        if n == 3:
+            halo_wait()
         compute(p)
         out_y(p)
         if n >= OUT_LAG:
@@ -345,7 +386,7 @@
     dma = pltpu.SemaphoreType.DMA
     out = pl.pallas_call(
         functools.partial(kernel, nz),
-        out_shape=jax.ShapeDtypeStruct((4, 5, nz, 8, 128), BF16),
+        out_shape=pltpu.VMEM((4, 5, nz, 8, 128), BF16),
         in_specs=[pl.BlockSpec(memory_space=pl.ANY)] * 3,
         out_specs=pl.BlockSpec(memory_space=pltpu.VMEM),
         scratch_shapes=[
@@ -363,18 +404,18 @@
             vm((8, 4, n_in), BF16),
             vm((nz, 8, 4, n_in), BF16),
             vm((8, blk, n_in), F32),
-            vm((32, half, n_in), BF16),
+            vm((4, 8, half, n_in), BF16),
             vm((5, 2, half, 128), BF16),
             vm((5, 8, blk, 128), BF16),
             vm((5, 8 * blk, 128), F32),
             vm((5, nz, 4, 8, 128), BF16),
             dma((5, nz)), dma((5, nz)), dma((nz,)), dma((nz,)), dma((nz,)), dma((nz,)),
-            dma((2, 4)), dma((2, 4)), dma((6,)), dma((6,)),
+            dma((3, 4)), dma((3, 4)), dma((2, 4, 4)), dma((2, 4, 4)),
             dma((5, 4)), dma((5, 4)), dma((5,)), dma((5,)), dma((2,)), dma((2,)), dma((2,)), dma((2,)),
             dma((5, 4)), dma((5, 4)), dma((5, nz)), dma((5, nz)), dma((5,)), dma((15,)),
         ],
         compiler_params=pltpu.CompilerParams(
-            collective_id=0, has_side_effects=True, vmem_limit_bytes=63 * 1024 * 1024
+            collective_id=0, has_side_effects=True, vmem_limit_bytes=56 * 1024 * 1024
         ),
         cost_estimate=pl.CostEstimate(
             flops=2 * 640 * n_in * n_in * 27, bytes_accessed=2 * v.size * 2, transcendentals=0

time: 59.4 us -> 51.5 us (0.87); the launches traced: 58.6 us -> 51.4 us
  Pallas kernels: 56.9 us -> 50.6 us
  local copies, waits for them, and re-layouts: 1.72 us -> 0.73 us
    pallas_call x1, Pallas kernels: 56.9 us -> 50.6 us  [shards(): pl.pallas_call(functools.partial(kernel, nz), out_shape=pltpu.VMEM((4, 5,...]
    unnamed x1, local copies, waits for them, and re-layouts: 1.72 us -> 0.73 us
where the time goes in v3:
time: 51.5 us; the launch traced here: 51.4 us
  Pallas kernels  50.6 us (98%)
  local copies, waits for them, and re-layouts  0.73 us (1%)
    pallas_call x1, Pallas kernels, shards(): pl.pallas_call(functools.partial(kernel, nz), out_shape=pltpu.VMEM((4, 5,...  50.6 us

profile of v3, /device:TPU:2, one launch (start us, length us, event | category | flops | bytes accessed | tf_op | source)
XLA Modules:
  0.0 51.4 jit_solution(6283889738454698170)
XLA Ops:
  0.0 50.6 %shard_map.37 = bf16[4,5,8,8,128]{4,3,2,1,0:T(8,128)(2,1)S(1)} custom-call(bf16[4,5,8,8,128]{4,3,2,1,0:T(8,128)(2,1)} %bitcast.5, bf16[27,4,256]{2,1,0:T(4,128)(2,1)} %bitcast.6, bf16[1,4]{1,0:T(2,128)(2,1)} %bitcast.7), custom_call_target="tpu_custom_call" | custom-call | flops 2264924160 | bytes 655360 | tf_op jit(solution)/shard_map/pallas_call | solution.py:387
  50.6 0.7 %copy.5 = bf16[4,5,64,128]{3,2,1,0:T(8,128)(2,1)} copy(bf16[4,5,64,128]{3,2,1,0:T(8,128)(2,1)S(1)} %bitcast.4) | data formatting | bytes 655360

commit v4 on v3

--- a/solution.py
+++ b/solution.py
@@ -12,7 +12,7 @@
 PLANES = (4, 0, 1, 2, 3)
 OUT_LAG = 3
 N1 = 5
-STEPS = "v4 v0 f1 f3 g0 v1 f2 v2 v3 g1 g3 c4 c0 g2 c1 c2 c3 h".split()
+STEPS = ("v4", "v0", "f1", "f3", "g0", "v1", "f2", "v2", "v3", "g1", "g3", "c4", "c0", "g2", "c1", "c2", "c3", "h")
 MESH = pl.DeviceIdType.MESH
 F32 = jnp.float32
 BF16 = jnp.bfloat16
@@ -24,8 +24,8 @@
 
 def kernel(
     nz, v_hbm, w_hbm, b_hbm, out,
-    v, b, fe, ed, rz, re, f, ge, g2, xz, X, ws, wz, wf, wt, O, oy, fo, oz,
-    s_vz, r_vz, s_ed, r_ed, s_wz, r_wz, s_wa, r_wa, s_wb, r_wb,
+    b, va, fe, et, rz, f, g2, xz, X, ws, wz, wf, wt, O, oy, fo, oz,
+    s_vz, r_vz, s_wz, r_wz, s_wa, r_wa, s_wb, r_wb,
     s_xy, r_xy, s_cc, r_cc, s_xh, r_xh, s_xf, r_xf, s_oy, r_oy, s_oz, r_oz, loc, loc_p,
 ):
     blk = 4 * nz
@@ -74,10 +74,10 @@
     peers += [sib]
     start = jnp.minimum(7 * x, 20)
     loads = [
-        local(v_hbm, v, loc.at[0]),
+        local(w_hbm.at[pl.ds(start, 7)], ws.at[pl.ds(0, 7)], loc.at[0]),
         local(b_hbm, b, loc.at[1]),
-        local(w_hbm.at[pl.ds(start, 7)], ws.at[pl.ds(0, 7)], loc.at[2]),
     ]
+    v_loads = [local(v_hbm.at[j], va.at[:, :, j], loc_p.at[15 + j]) for j in range(4)]
     for p in peers:
         pl.semaphore_signal(bar, inc=1, device_id=p, device_id_type=MESH)
 
@@ -102,36 +102,34 @@
     ws[7] = jnp.broadcast_to(col, ws.shape[1:]).astype(BF16)
 
     loads[0].wait()
-    for j in range(4):
-        for p in range(5):
-            base = (j * 5 + p) * nz * 8
-            for k in range(nz):
-                fe[base + 8 * k:base + 8 * k + 8, :] = v[j, p, k].astype(F32)
-    zero_edge = jnp.zeros((20, 128), BF16)
-    ed[0, 0] = zero_edge
-    ed[nz - 1, 1] = zero_edge
-    for k in range(1, nz):
-        ed[k, 0] = fe[pl.ds(8 * k - 1, 20, stride=8 * nz), :].astype(BF16)
-        ed[k - 1, 1] = fe[pl.ds(8 * k, 20, stride=8 * nz), :].astype(BF16)
-    loads[2].wait()
 
     pl.semaphore_wait(bar, len(peers))
 
     for k in z_order:
         sent.append(send(ws, wz.at[z], s_wz.at[k], r_wz.at[k], at(zk(k), y, c, x)))
     own_w = local(ws, wz.at[z], loc.at[3])
-    for k in z_order:
-        d = zk(k)
-        sent.append(send(ed.at[d], re.at[z], s_ed.at[k], r_ed.at[k], at(d, y, c, x)))
-    own_e = local(ed.at[z], re.at[z], loc.at[4])
+    for cp in v_loads:
+        cp.wait()
     own_v = {}
     for p in PLANES:
+        for d in range(nz):
+            for j in range(4):
+                r0 = (d * 4 + j) * 8
+                fe[p, r0:r0 + 8, :] = va[p, d, j].astype(F32)
+        for d in range(nz):
+            et[p, d, 0:4, :] = (
+                fe[p, pl.ds((d - 1) * 32 + 7, 4, stride=8), :] if d else jnp.zeros((4, 128), F32)
+            )
+            et[p, d, 4:8, :] = (
+                fe[p, pl.ds((d + 1) * 32, 4, stride=8), :] if d < nz - 1 else jnp.zeros((4, 128), F32)
+            )
+            va[p, d, 4] = et[p, d].astype(BF16)
         for k in z_order:
             d = zk(k)
             sent.append(
-                send(v.at[:, p, d], rz.at[p, z], s_vz.at[p, k], r_vz.at[p, k], at(d, y, c, x))
-            )
-        own_v[p] = local(v.at[:, p, z], rz.at[p, z], loc_p.at[p])
+                send(va.at[p, d], rz.at[p, z], s_vz.at[p, k], r_vz.at[p, k], at(d, y, c, x))
+            )
+        own_v[p] = local(va.at[p, z], rz.at[p, z], loc_p.at[p])
 
     own_w.wait()
     for k in z_order[::-1]:
@@ -160,12 +158,12 @@
         return wt.at[g, pl.ds(N1, 7 - N1), part_rows(yy, h), :]
 
     def w3(yy):
-        return wt.at[x, 7, rows(yy), :]
+        return wt.at[x, 7, rows(yy), pl.ds(0, min(128, n_in))]
 
     def xk(k):
         return lax.rem(x + k + NXT, NXT)
 
-    for k in (2, 1, 3):
+    for k in (1, 3, 2):
         sent.append(send(w1(x, y), w1(x, y), s_wa.at[0, k], r_wa.at[0, k], at(z, yk(k), c, x)))
         sent.append(send(w2(x, y), w2(x, y), s_wa.at[1, k], r_wa.at[1, k], at(z, y, c, xk(k))))
         sent.append(send(w3(y), w3(y), s_wa.at[2, k], r_wa.at[2, k], at(z, yk(k), c, x)))
@@ -213,6 +211,12 @@
             for j in range(4):
                 r0 = (s * 4 + j) * 8
                 f[p, r0:r0 + 8, :] = rz[p, s, j].astype(F32)
+        for s in range(nz):
+            e = rz[p, s, 4].astype(F32)
+            g2[p, 4 * s:4 * s + 4, :] = e[0:4]
+            g2[5 + p, 4 * s:4 * s + 4, :] = e[4:8]
+        xz[p, 0] = g2[p].astype(BF16)
+        xz[p, 9] = g2[5 + p].astype(BF16)
         for r in range(8):
             xz[p, r + 1] = f[p, pl.ds(r, blk, stride=8), :].astype(BF16)
         for k in (2, 1, 3):
@@ -224,18 +228,6 @@
                 )
             )
         own_y[p] = local(xz.at[p, pl.ds(2 * y, 4)], x_part(p, y), loc_p.at[5 + p])
-
-    own_e.wait()
-    for k in z_order[::-1]:
-        recv(re.at[zk(-k)], r_ed.at[k])
-    for s in range(nz):
-        for side in range(2):
-            ge[s, side] = re[s, side].astype(F32)
-    for side in range(2):
-        for p in range(5):
-            for s in range(nz):
-                g2[side * 5 + p, 4 * s:4 * s + 4, :] = ge[s, side, pl.ds(p, 4, stride=5), :]
-            xz[p, 9 * side] = g2[side * 5 + p].astype(BF16)
 
     def share(p):
         own_y[p].wait()
@@ -390,14 +382,12 @@
         in_specs=[pl.BlockSpec(memory_space=pl.ANY)] * 3,
         out_specs=pl.BlockSpec(memory_space=pltpu.VMEM),
         scratch_shapes=[
-            vm((4, 5, nz, 8, 128), BF16),
             vm((1, 4), BF16),
-            vm((20 * 8 * nz, 128), F32),
-            vm((nz, 2, 20, 128), BF16),
-            vm((5, nz, 4, 8, 128), BF16),
-            vm((nz, 2, 20, 128), BF16),
+            vm((5, nz, 5, 8, 128), BF16),
             vm((5, blk * 8, 128), F32),
-            vm((nz, 2, 20, 128), F32),
+            vm((5, nz, 8, 128), F32),
+            vm((5, nz, 5, 8, 128), BF16),
+            vm((5, blk * 8, 128), F32),
             vm((10, blk, 128), F32),
             vm((5, 10, blk, 128), BF16),
             vm((2, 7, 4, half, 128), BF16),
@@ -409,10 +399,10 @@
             vm((5, 8, blk, 128), BF16),
             vm((5, 8 * blk, 128), F32),
             vm((5, nz, 4, 8, 128), BF16),
-            dma((5, nz)), dma((5, nz)), dma((nz,)), dma((nz,)), dma((nz,)), dma((nz,)),
+            dma((5, nz)), dma((5, nz)), dma((nz,)), dma((nz,)),
             dma((3, 4)), dma((3, 4)), dma((2, 4, 4)), dma((2, 4, 4)),
             dma((5, 4)), dma((5, 4)), dma((5,)), dma((5,)), dma((2,)), dma((2,)), dma((2,)), dma((2,)),
-            dma((5, 4)), dma((5, 4)), dma((5, nz)), dma((5, nz)), dma((5,)), dma((15,)),
+            dma((5, 4)), dma((5, 4)), dma((5, nz)), dma((5, nz)), dma((5,)), dma((19,)),
         ],
         compiler_params=pltpu.CompilerParams(
             collective_id=0, has_side_effects=True, vmem_limit_bytes=56 * 1024 * 1024

time: 51.5 us -> 50.9 us (0.988); the launches traced: 51.4 us -> 50.2 us
  Pallas kernels: 50.6 us -> 49.5 us
    pallas_call x1, Pallas kernels: 50.6 us -> 49.5 us  [shards(): pl.pallas_call(functools.partial(kernel, nz), out_shape=pltpu.VMEM((4, 5,...]
where the time goes in v4:
time: 50.9 us; the launch traced here: 50.2 us
  Pallas kernels  49.5 us (97%)
  local copies, waits for them, and re-layouts  0.73 us (1%)
    pallas_call x1, Pallas kernels, shards(): pl.pallas_call(functools.partial(kernel, nz), out_shape=pltpu.VMEM((4, 5,...  49.5 us

profile of v4, /device:TPU:2, one launch (start us, length us, event | category | flops | bytes accessed | tf_op | source)
XLA Modules:
  0.0 50.2 jit_solution(3921519538790471160)
XLA Ops:
  0.0 49.5 %shard_map.37 = bf16[4,5,8,8,128]{4,3,2,1,0:T(8,128)(2,1)S(1)} custom-call(bf16[4,5,8,8,128]{4,3,2,1,0:T(8,128)(2,1)} %bitcast.5, bf16[27,4,256]{2,1,0:T(4,128)(2,1)} %bitcast.6, bf16[1,4]{1,0:T(2,128)(2,1)} %bitcast.7), custom_call_target="tpu_custom_call" | custom-call | flops 2264924160 | bytes 655360 | tf_op jit(solution)/shard_map/pallas_call | solution.py:379
  49.5 0.7 %copy.5 = bf16[4,5,64,128]{3,2,1,0:T(8,128)(2,1)} copy(bf16[4,5,64,128]{3,2,1,0:T(8,128)(2,1)S(1)} %bitcast.4) | data formatting | bytes 655360

commit v5 on v4

--- a/solution.py
+++ b/solution.py
@@ -25,8 +25,8 @@
 def kernel(
     nz, v_hbm, w_hbm, b_hbm, out,
     b, va, fe, et, rz, f, g2, xz, X, ws, wz, wf, wt, O, oy, fo, oz,
-    s_vz, r_vz, s_wz, r_wz, s_wa, r_wa, s_wb, r_wb,
-    s_xy, r_xy, s_cc, r_cc, s_xh, r_xh, s_xf, r_xf, s_oy, r_oy, s_oz, r_oz, loc, loc_p,
+    s_vz, r_vz, s_wz, r_wz, s_wa, r_wa, s_w3, r_w3, s_wb, r_wb, r_wh,
+    s_xy, r_xy, s_cc, r_cc, s_xh, r_xh, s_xf, r_xf, s_oy, r_oy, s_oz, r_oz, loc,
 ):
     blk = 4 * nz
     half = NYT * blk
@@ -64,7 +64,6 @@
         cp.start()
         return cp
 
-    sent = []
     z_order = sorted(range(1, nz), key=lambda k: -min(k, nz - k))
 
     bar = pltpu.get_barrier_semaphore()
@@ -77,7 +76,8 @@
         local(w_hbm.at[pl.ds(start, 7)], ws.at[pl.ds(0, 7)], loc.at[0]),
         local(b_hbm, b, loc.at[1]),
     ]
-    v_loads = [local(v_hbm.at[j], va.at[:, :, j], loc_p.at[15 + j]) for j in range(4)]
+    for j in range(4):
+        local(v_hbm.at[j], va.at[:, :, j], loc.at[2])
     for p in peers:
         pl.semaphore_signal(bar, inc=1, device_id=p, device_id_type=MESH)
 
@@ -106,11 +106,9 @@
     pl.semaphore_wait(bar, len(peers))
 
     for k in z_order:
-        sent.append(send(ws, wz.at[z], s_wz.at[k], r_wz.at[k], at(zk(k), y, c, x)))
-    own_w = local(ws, wz.at[z], loc.at[3])
-    for cp in v_loads:
-        cp.wait()
-    own_v = {}
+        send(ws, wz.at[z], s_wz, r_wz, at(zk(k), y, c, x))
+    local(ws, wz.at[z], r_wz)
+    recv(va.at[:, :, pl.ds(0, 4)], loc.at[2])
     for p in PLANES:
         for d in range(nz):
             for j in range(4):
@@ -126,14 +124,12 @@
             va[p, d, 4] = et[p, d].astype(BF16)
         for k in z_order:
             d = zk(k)
-            sent.append(
-                send(va.at[p, d], rz.at[p, z], s_vz.at[p, k], r_vz.at[p, k], at(d, y, c, x))
-            )
-        own_v[p] = local(va.at[p, z], rz.at[p, z], loc_p.at[p])
-
-    own_w.wait()
-    for k in z_order[::-1]:
-        recv(wz.at[zk(-k)], r_wz.at[k])
+            send(
+                *(va.at[p, d], rz.at[p, z], s_vz, r_vz.at[p], at(d, y, c, x))
+            )
+        local(va.at[p, z], rz.at[p, z], r_vz.at[p])
+
+    recv(wz, r_wz)
     for t in range(8):
         for s in range(nz):
             wf[t, 4 * s:4 * s + 4, :] = wz[s, t].astype(F32)
@@ -164,49 +160,45 @@
         return lax.rem(x + k + NXT, NXT)
 
     for k in (1, 3, 2):
-        sent.append(send(w1(x, y), w1(x, y), s_wa.at[0, k], r_wa.at[0, k], at(z, yk(k), c, x)))
-        sent.append(send(w2(x, y), w2(x, y), s_wa.at[1, k], r_wa.at[1, k], at(z, y, c, xk(k))))
-        sent.append(send(w3(y), w3(y), s_wa.at[2, k], r_wa.at[2, k], at(z, yk(k), c, x)))
+        send(w1(x, y), w1(x, y), s_wa, r_wa.at[0, k - 1], at(z, yk(k), c, x))
+        send(w2(x, y), w2(x, y), s_wa, r_wa.at[1, k - 1], at(z, y, c, xk(k)))
+        send(w3(y), w3(y), s_w3, r_w3, at(z, yk(k), c, x))
 
     def forward(q):
         yq, xq = yk(-q), xk(-q)
         if q:
-            recv(w1(x, yq), r_wa.at[0, q])
+            recv(w1(x, yq), r_wa.at[0, q - 1])
         for k in (1, 3):
             to = at(z, y, c, xk(k))
-            sent.append(send(w1(x, yq), w1(x, yq), s_wb.at[0, q, k], r_wb.at[0, q, k], to))
+            send(w1(x, yq), w1(x, yq), s_wb, r_wb.at[0, q, k // 2], to)
         if q:
-            recv(w2(xq, y), r_wa.at[1, q])
+            recv(w2(xq, y), r_wa.at[1, q - 1])
         for k in (1, 3):
             to = at(z, yk(k), c, x)
-            sent.append(send(w2(xq, y), w2(xq, y), s_wb.at[1, q, k], r_wb.at[1, q, k], to))
+            send(w2(xq, y), w2(xq, y), s_wb, r_wb.at[1, q, k // 2], to)
 
     def pass_on(q):
         yq, xq = yk(-q), xk(-q)
-        recv(w1(xk(-1), yq), r_wb.at[0, q, 1])
+        recv(w1(xk(-1), yq), r_wb.at[0, q, 0])
         half0 = w1(xk(-1), yq, 0)
-        sent.append(send(half0, half0, s_wb.at[0, q, 2], r_wb.at[0, q, 2], at(z, y, c, xk(1))))
-        recv(w1(xk(1), yq), r_wb.at[0, q, 3])
+        send(half0, half0, s_wb, r_wh, at(z, y, c, xk(1)))
+        recv(w1(xk(1), yq), r_wb.at[0, q, 1])
         half1 = w1(xk(1), yq, 1)
-        sent.append(send(half1, half1, s_wb.at[0, q, 0], r_wb.at[0, q, 0], at(z, y, c, xk(-1))))
-        recv(w2(xq, yk(-1)), r_wb.at[1, q, 1])
+        send(half1, half1, s_wb, r_wh, at(z, y, c, xk(-1)))
+        recv(w2(xq, yk(-1)), r_wb.at[1, q, 0])
         half2 = w2(xq, yk(-1), 0)
-        sent.append(send(half2, half2, s_wb.at[1, q, 2], r_wb.at[1, q, 2], at(z, yk(1), c, x)))
-        recv(w2(xq, yk(1)), r_wb.at[1, q, 3])
+        send(half2, half2, s_wb, r_wh, at(z, yk(1), c, x))
+        recv(w2(xq, yk(1)), r_wb.at[1, q, 1])
         half3 = w2(xq, yk(1), 1)
-        sent.append(send(half3, half3, s_wb.at[1, q, 0], r_wb.at[1, q, 0], at(z, yk(-1), c, x)))
+        send(half3, half3, s_wb, r_wh, at(z, yk(-1), c, x))
 
     forward(0)
 
     def x_part(p, yy):
         return X.at[c, p + 1, :, pl.ds(pl.multiple_of(yy * blk, blk), blk), :]
 
-    own_y = {}
-
     def volume_y(p):
-        own_v[p].wait()
-        for k in z_order[::-1]:
-            recv(rz.at[p, zk(-k)], r_vz.at[p, k])
+        recv(rz.at[p], r_vz.at[p])
         for s in range(nz):
             for j in range(4):
                 r0 = (s * 4 + j) * 8
@@ -221,18 +213,16 @@
             xz[p, r + 1] = f[p, pl.ds(r, blk, stride=8), :].astype(BF16)
         for k in (2, 1, 3):
             d = yk(k)
-            sent.append(
-                send(
-                    xz.at[p, pl.ds(2 * d, 4)], x_part(p, y), s_xy.at[p, k], r_xy.at[p, k],
+            send(
+                *(
+                    xz.at[p, pl.ds(2 * d, 4)], x_part(p, y), s_xy, r_xy.at[p],
                     at(z, d, c, x),
                 )
             )
-        own_y[p] = local(xz.at[p, pl.ds(2 * y, 4)], x_part(p, y), loc_p.at[5 + p])
+        local(xz.at[p, pl.ds(2 * y, 4)], x_part(p, y), r_xy.at[p])
 
     def share(p):
-        own_y[p].wait()
-        for k in range(1, NYT):
-            recv(x_part(p, yk(-k)), r_xy.at[p, k])
+        recv(X.at[c, p + 1], r_xy.at[p])
         if p == 4:
             @pl.when(x < NXT - 1)
             def _():
@@ -241,7 +231,7 @@
             @pl.when(x > 0)
             def _():
                 send(X.at[c, 1], X.at[c, 6], s_xh.at[1], r_xh.at[1], left)
-        sent.append(send(X.at[c, p + 1], X.at[c, p + 1], s_cc.at[p], r_cc.at[p], sib))
+        send(X.at[c, p + 1], X.at[c, p + 1], s_cc, r_cc, sib)
 
     def halo():
         @pl.when(x > 0)
@@ -266,15 +256,10 @@
         else:
             halo()
 
-    for p in PLANES:
-        recv(X.at[1 - c, p + 1], r_cc.at[p])
-
-    for q in range(NXT):
-        for h, k in ((0, 2), (1, 0)):
-            recv(w1(xk(2), yk(-q), h), r_wb.at[0, q, k])
-            recv(w2(xk(-q), yk(2), h), r_wb.at[1, q, k])
-    for k in range(1, NYT):
-        recv(w3(yk(-k)), r_wa.at[2, k])
+    recv(X.at[1 - c, pl.ds(1, 5)], r_cc)
+
+    recv(wt.at[0, pl.ds(0, 7)], r_wh)
+    recv(wt.at[pl.ds(0, 3), 7, rows(y), pl.ds(0, min(128, n_in))], r_w3)
 
     def halo_wait():
         @pl.when(x > 0)
@@ -313,30 +298,28 @@
     def out_y(p):
         for k in (2, 1, 3):
             d = yk(k)
-            sent.append(
-                send(
+            send(
+                *(
                     O.at[p, :, pl.ds(pl.multiple_of(d * blk, blk), blk), :],
                     oy.at[p, pl.ds(2 * y, 2)],
-                    s_oy.at[p, k], r_oy.at[p, k], at(z, d, c, x),
+                    s_oy, r_oy.at[p], at(z, d, c, x),
                 )
             )
         oy[p, pl.ds(2 * y, 2)] = O[p, :, pl.ds(yoff, blk), :]
 
     def out_z(p):
-        for k in range(1, NYT):
-            recv(oy.at[p, pl.ds(2 * yk(-k), 2)], r_oy.at[p, k])
+        recv(oy.at[p, pl.ds(0, 6)], r_oy.at[p])
         for r in range(8):
             fo[p, blk * r:blk * r + blk, :] = oy[p, r].astype(F32)
         for m in range(blk):
             oz[p, m // 4, m % 4] = fo[p, pl.ds(m, 8, stride=blk), :].astype(BF16)
         for k in z_order:
             d = zk(k)
-            sent.append(
-                send(oz.at[p, d], out.at[:, p, z], s_oz.at[p, k], r_oz.at[p, k], at(d, y, c, x))
-            )
-        return local(oz.at[p, z], out.at[:, p, z], loc_p.at[10 + p])
-
-    finals = []
+            send(
+                *(oz.at[p, d], out.at[:, p, z], s_oz, r_oz, at(d, y, c, x))
+            )
+        local(oz.at[p, z], out.at[:, p, z], r_oz)
+
     order = [1, 2, 3, 0, 4]
     for n, p in enumerate(order):
         if n == 3:
@@ -344,17 +327,20 @@
         compute(p)
         out_y(p)
         if n >= OUT_LAG:
-            finals.append(out_z(order[n - OUT_LAG]))
+            out_z(order[n - OUT_LAG])
     for p in order[5 - OUT_LAG:]:
-        finals.append(out_z(p))
-
-    for cp in finals:
-        cp.wait()
-    for p in order:
-        for k in range(1, nz):
-            recv(out.at[:, p, zk(-k)], r_oz.at[p, k])
-    for cp in sent:
-        cp.wait_send()
+        out_z(p)
+
+    recv(out, r_oz)
+    recv(wz.at[pl.ds(0, nz - 1)], s_wz)
+    recv(rz.at[:, pl.ds(0, nz - 1)], s_vz)
+    recv(wt.at[pl.ds(0, 3), pl.ds(0, 7), rows(y), :], s_wa)
+    recv(wt.at[pl.ds(0, 3), 7, rows(y), pl.ds(0, min(128, n_in))], s_w3)
+    recv(wt.at[pl.ds(0, 3), pl.ds(0, 7)], s_wb)
+    recv(X.at[0, pl.ds(0, 5), :, pl.ds(0, 3 * blk), :], s_xy)
+    recv(X.at[0, pl.ds(1, 5)], s_cc)
+    recv(O.at[:, :, pl.ds(0, 3 * blk), :], s_oy)
+    recv(oz.at[:, pl.ds(0, nz - 1)], s_oz)
 
     @pl.when(x < NXT - 1)
     def _():
@@ -399,10 +385,10 @@
             vm((5, 8, blk, 128), BF16),
             vm((5, 8 * blk, 128), F32),
             vm((5, nz, 4, 8, 128), BF16),
-            dma((5, nz)), dma((5, nz)), dma((nz,)), dma((nz,)),
-            dma((3, 4)), dma((3, 4)), dma((2, 4, 4)), dma((2, 4, 4)),
-            dma((5, 4)), dma((5, 4)), dma((5,)), dma((5,)), dma((2,)), dma((2,)), dma((2,)), dma((2,)),
-            dma((5, 4)), dma((5, 4)), dma((5, nz)), dma((5, nz)), dma((5,)), dma((19,)),
+            dma(()), dma((5,)), dma(()), dma(()),
+            dma(()), dma((2, 3)), dma(()), dma(()), dma(()), dma((2, 4, 2)), dma(()),
+            dma(()), dma((5,)), dma(()), dma(()), dma((2,)), dma((2,)), dma((2,)), dma((2,)),
+            dma(()), dma((5,)), dma(()), dma(()), dma((3,)),
         ],
         compiler_params=pltpu.CompilerParams(
             collective_id=0, has_side_effects=True, vmem_limit_bytes=56 * 1024 * 1024

time: 50.9 us -> 47.7 us (0.937)
  Pallas kernels: 49.5 us -> 46.2 us
    pallas_call x1, Pallas kernels: 49.5 us -> 46.2 us  [shards(): pl.pallas_call(functools.partial(kernel, nz), out_shape=pltpu.VMEM((4, 5,...]
where the time goes in v5:
time: 47.7 us; the launch traced here: 47 us
  Pallas kernels  46.2 us (97%)
  local copies, waits for them, and re-layouts  0.73 us (2%)
    pallas_call x1, Pallas kernels, shards(): pl.pallas_call(functools.partial(kernel, nz), out_shape=pltpu.VMEM((4, 5,...  46.2 us

profile of v5, /device:TPU:2, one launch (start us, length us, event | category | flops | bytes accessed | tf_op | source)
XLA Modules:
  0.0 47.0 jit_solution(427320624570920764)
XLA Ops:
  0.0 46.2 %shard_map.37 = bf16[4,5,8,8,128]{4,3,2,1,0:T(8,128)(2,1)S(1)} custom-call(bf16[4,5,8,8,128]{4,3,2,1,0:T(8,128)(2,1)} %bitcast.5, bf16[27,4,256]{2,1,0:T(4,128)(2,1)} %bitcast.6, bf16[1,4]{1,0:T(2,128)(2,1)} %bitcast.7), custom_call_target="tpu_custom_call" | custom-call | flops 2264924160 | bytes 655360 | tf_op jit(solution)/shard_map/pallas_call | solution.py:365
  46.2 0.7 %copy.5 = bf16[4,5,64,128]{3,2,1,0:T(8,128)(2,1)} copy(bf16[4,5,64,128]{3,2,1,0:T(8,128)(2,1)S(1)} %bitcast.4) | data formatting | bytes 655360

commit v6 on v5

--- a/solution.py
+++ b/solution.py
@@ -10,7 +10,6 @@
 NYT = 4
 NXT = 4
 PLANES = (4, 0, 1, 2, 3)
-OUT_LAG = 3
 N1 = 5
 STEPS = ("v4", "v0", "f1", "f3", "g0", "v1", "f2", "v2", "v3", "g1", "g3", "c4", "c0", "g2", "c1", "c2", "c3", "h")
 MESH = pl.DeviceIdType.MESH
@@ -24,9 +23,9 @@
 
 def kernel(
     nz, v_hbm, w_hbm, b_hbm, out,
-    b, va, fe, et, rz, f, g2, xz, X, ws, wz, wf, wt, O, oy, fo, oz,
+    b, va, fe, et, rz, f, g2, xz, X, ws, wz, wf, wt, O, oy, fo, oz, fz, oz1, iz, fy, oy1, iy, fl,
     s_vz, r_vz, s_wz, r_wz, s_wa, r_wa, s_w3, r_w3, s_wb, r_wb, r_wh,
-    s_xy, r_xy, s_cc, r_cc, s_xh, r_xh, s_xf, r_xf, s_oy, r_oy, s_oz, r_oz, loc,
+    s_xy, r_xy, s_cc, r_cc, s_xh, r_xh, s_xf, r_xf, s_oy, r_oy, s_oz, r_oz, s_z1, r_z1, s_y1, r_y1, loc,
 ):
     blk = 4 * nz
     half = NYT * blk
@@ -320,18 +319,64 @@
             )
         local(oz.at[p, z], out.at[:, p, z], r_oz)
 
-    order = [1, 2, 3, 0, 4]
-    for n, p in enumerate(order):
-        if n == 3:
-            halo_wait()
-        compute(p)
-        out_y(p)
-        if n >= OUT_LAG:
-            out_z(order[n - OUT_LAG])
-    for p in order[5 - OUT_LAG:]:
-        out_z(p)
-
-    recv(out, r_oz)
+    def first_z(p, i):
+        for r in range(2):
+            fo[p, half * r:half * r + half, :] = O[p, r].astype(F32)
+            for zz in range(nz):
+                for yy in range(NYT):
+                    r0 = half * r + blk * yy + 4 * zz
+                    fz[i, zz, r, 4 * yy:4 * yy + 4, :] = fo[p, r0:r0 + 4, :]
+                oz1[i, zz, r] = fz[i, zz, r].astype(BF16)
+        for k in z_order:
+            d = zk(k)
+            send(oz1.at[i, d], iz.at[i, z], s_z1, r_z1.at[i], at(d, y, c, x))
+        local(oz1.at[i, z], iz.at[i, z], r_z1.at[i])
+
+    def then_y(i):
+        recv(iz.at[i], r_z1.at[i])
+        for zz in range(nz):
+            for r in range(2):
+                rows16 = iz[i, zz, r].astype(F32)
+                r0 = (zz * 2 + r) * 4
+                for yy in range(NYT):
+                    fy[i, yy, r0:r0 + 4, :] = rows16[4 * yy:4 * yy + 4]
+        for yy in range(NYT):
+            oy1[i, yy] = fy[i, yy].astype(BF16)
+        for k in (2, 1, 3):
+            d = yk(k)
+            send(oy1.at[i, d], iy.at[i, y], s_y1, r_y1.at[i], at(z, d, c, x))
+        local(oy1.at[i, y], iy.at[i, y], r_y1.at[i])
+
+    def finish(p, i):
+        recv(iy.at[i], r_y1.at[i])
+        for yy in range(NYT):
+            block = iy[i, yy].astype(F32)
+            for zz in range(nz):
+                fl[i, zz, 8 * yy:8 * yy + 8, :] = block[8 * zz:8 * zz + 8]
+        for zz in range(nz):
+            for j in range(4):
+                out[j, p, zz] = fl[i, zz, pl.ds(j, 8, stride=4), :].astype(BF16)
+
+    compute(1)
+    first_z(1, 0)
+    compute(2)
+    first_z(2, 1)
+    compute(3)
+    out_y(3)
+    halo_wait()
+    compute(0)
+    out_y(0)
+    compute(4)
+    out_y(4)
+    then_y(0)
+    out_z(3)
+    then_y(1)
+    out_z(0)
+    out_z(4)
+    finish(1, 0)
+    finish(2, 1)
+
+    recv(out.at[:, pl.ds(0, 3)], r_oz)
     recv(wz.at[pl.ds(0, nz - 1)], s_wz)
     recv(rz.at[:, pl.ds(0, nz - 1)], s_vz)
     recv(wt.at[pl.ds(0, 3), pl.ds(0, 7), rows(y), :], s_wa)
@@ -339,8 +384,10 @@
     recv(wt.at[pl.ds(0, 3), pl.ds(0, 7)], s_wb)
     recv(X.at[0, pl.ds(0, 5), :, pl.ds(0, 3 * blk), :], s_xy)
     recv(X.at[0, pl.ds(1, 5)], s_cc)
-    recv(O.at[:, :, pl.ds(0, 3 * blk), :], s_oy)
-    recv(oz.at[:, pl.ds(0, nz - 1)], s_oz)
+    recv(O.at[pl.ds(0, 3), :, pl.ds(0, 3 * blk), :], s_oy)
+    recv(oz.at[pl.ds(0, 3), pl.ds(0, nz - 1)], s_oz)
+    recv(oz1.at[:, pl.ds(0, nz - 1)], s_z1)
+    recv(oy1.at[:, pl.ds(0, 3)], s_y1)
 
     @pl.when(x < NXT - 1)
     def _():
@@ -385,10 +432,17 @@
             vm((5, 8, blk, 128), BF16),
             vm((5, 8 * blk, 128), F32),
             vm((5, nz, 4, 8, 128), BF16),
+            vm((2, nz, 2, 16, 128), F32),
+            vm((2, nz, 2, 16, 128), BF16),
+            vm((2, nz, 2, 16, 128), BF16),
+            vm((2, NYT, 8 * nz, 128), F32),
+            vm((2, NYT, 8 * nz, 128), BF16),
+            vm((2, NYT, 8 * nz, 128), BF16),
+            vm((2, nz, 32, 128), F32),
             dma(()), dma((5,)), dma(()), dma(()),
             dma(()), dma((2, 3)), dma(()), dma(()), dma(()), dma((2, 4, 2)), dma(()),
             dma(()), dma((5,)), dma(()), dma(()), dma((2,)), dma((2,)), dma((2,)), dma((2,)),
-            dma(()), dma((5,)), dma(()), dma(()), dma((3,)),
+            dma(()), dma((5,)), dma(()), dma(()), dma(()), dma((2,)), dma(()), dma((2,)), dma((3,)),
         ],
         compiler_params=pltpu.CompilerParams(
             collective_id=0, has_side_effects=True, vmem_limit_bytes=56 * 1024 * 1024

time: 47.7 us -> 46.8 us (0.981); the launches traced: 47 us -> 46.6 us
  no operation moved by 1% of the time
where the time goes in v6:
time: 46.8 us; the launch traced here: 46.6 us
  Pallas kernels  45.9 us (98%)
  local copies, waits for them, and re-layouts  0.73 us (2%)
    pallas_call x1, Pallas kernels, shards(): pl.pallas_call(functools.partial(kernel, nz), out_shape=pltpu.VMEM((4, 5,...  45.9 us

profile of v6, /device:TPU:2, one launch (start us, length us, event | category | flops | bytes accessed | tf_op | source)
XLA Modules:
  0.0 46.6 jit_solution(13754468441326012338)
XLA Ops:
  0.0 45.9 %shard_map.37 = bf16[4,5,8,8,128]{4,3,2,1,0:T(8,128)(2,1)S(1)} custom-call(bf16[4,5,8,8,128]{4,3,2,1,0:T(8,128)(2,1)} %bitcast.5, bf16[27,4,256]{2,1,0:T(4,128)(2,1)} %bitcast.6, bf16[1,4]{1,0:T(2,128)(2,1)} %bitcast.7), custom_call_target="tpu_custom_call" | custom-call | flops 2264924160 | bytes 655360 | tf_op jit(solution)/shard_map/pallas_call | solution.py:412
  45.9 0.7 %copy.5 = bf16[4,5,64,128]{3,2,1,0:T(8,128)(2,1)} copy(bf16[4,5,64,128]{3,2,1,0:T(8,128)(2,1)S(1)} %bitcast.4) | data formatting | bytes 655360

commit v7 on v6

--- a/solution.py
+++ b/solution.py
@@ -70,6 +70,8 @@
     peers += [at(z, yk(k), c, x) for k in range(1, NYT)]
     peers += [at(z, y, c, lax.rem(x + k, NXT)) for k in range(1, NXT)]
     peers += [sib]
+    for p in peers:
+        pl.semaphore_signal(bar, inc=1, device_id=p, device_id_type=MESH)
     start = jnp.minimum(7 * x, 20)
     loads = [
         local(w_hbm.at[pl.ds(start, 7)], ws.at[pl.ds(0, 7)], loc.at[0]),
@@ -77,8 +79,6 @@
     ]
     for j in range(4):
         local(v_hbm.at[j], va.at[:, :, j], loc.at[2])
-    for p in peers:
-        pl.semaphore_signal(bar, inc=1, device_id=p, device_id_type=MESH)
 
     @pl.when(x == 0)
     def _():
@@ -129,11 +129,11 @@
         local(va.at[p, z], rz.at[p, z], r_vz.at[p])
 
     recv(wz, r_wz)
-    for t in range(8):
+    yoff = pl.multiple_of(y * blk, blk)
+
+    def arrange(t):
         for s in range(nz):
             wf[t, 4 * s:4 * s + 4, :] = wz[s, t].astype(F32)
-    yoff = pl.multiple_of(y * blk, blk)
-    for t in range(8):
         wt[x, t, pl.ds(yoff, blk), :] = jnp.dot(
             wf[t].astype(BF16), perm, preferred_element_type=F32
         ).astype(BF16)
@@ -158,8 +158,13 @@
     def xk(k):
         return lax.rem(x + k + NXT, NXT)
 
+    for t in range(N1):
+        arrange(t)
     for k in (1, 3, 2):
         send(w1(x, y), w1(x, y), s_wa, r_wa.at[0, k - 1], at(z, yk(k), c, x))
+    for t in range(N1, 8):
+        arrange(t)
+    for k in (1, 3, 2):
         send(w2(x, y), w2(x, y), s_wa, r_wa.at[1, k - 1], at(z, y, c, xk(k)))
         send(w3(y), w3(y), s_w3, r_w3, at(z, yk(k), c, x))
 

time: 46.8 us -> 46.8 us (level)
  no operation moved by 1% of the time
where the time goes in v7:
time: 46.8 us; the launch traced here: 46.6 us
  Pallas kernels  45.9 us (98%)
  local copies, waits for them, and re-layouts  0.73 us (2%)
    pallas_call x1, Pallas kernels, shards(): pl.pallas_call(functools.partial(kernel, nz), out_shape=pltpu.VMEM((4, 5,...  45.9 us

profile of v7, /device:TPU:2, one launch (start us, length us, event | category | flops | bytes accessed | tf_op | source)
XLA Modules:
  0.0 46.6 jit_solution(2419095590593936624)
XLA Ops:
  0.0 45.9 %shard_map.37 = bf16[4,5,8,8,128]{4,3,2,1,0:T(8,128)(2,1)S(1)} custom-call(bf16[4,5,8,8,128]{4,3,2,1,0:T(8,128)(2,1)} %bitcast.5, bf16[27,4,256]{2,1,0:T(4,128)(2,1)} %bitcast.6, bf16[1,4]{1,0:T(2,128)(2,1)} %bitcast.7), custom_call_target="tpu_custom_call" | custom-call | flops 2264924160 | bytes 655360 | tf_op jit(solution)/shard_map/pallas_call | solution.py:417
  45.9 0.7 %copy.5 = bf16[4,5,64,128]{3,2,1,0:T(8,128)(2,1)} copy(bf16[4,5,64,128]{3,2,1,0:T(8,128)(2,1)S(1)} %bitcast.4) | data formatting | bytes 655360

commit v8 on v7

--- a/solution.py
+++ b/solution.py
@@ -373,10 +373,10 @@
     out_y(0)
     compute(4)
     out_y(4)
+    out_z(3)
     then_y(0)
-    out_z(3)
+    out_z(0)
     then_y(1)
-    out_z(0)
     out_z(4)
     finish(1, 0)
     finish(2, 1)

time: 46.8 us -> 46.7 us (level)
  no operation moved by 1% of the time
where the time goes in v8:
time: 46.7 us; the launch traced here: 46.6 us
  Pallas kernels  45.9 us (98%)
  local copies, waits for them, and re-layouts  0.73 us (2%)
    pallas_call x1, Pallas kernels, shards(): pl.pallas_call(functools.partial(kernel, nz), out_shape=pltpu.VMEM((4, 5,...  45.9 us

profile of v8, /device:TPU:2, one launch (start us, length us, event | category | flops | bytes accessed | tf_op | source)
XLA Modules:
  0.0 46.6 jit_solution(16277841238607836325)
XLA Ops:
  0.0 45.9 %shard_map.37 = bf16[4,5,8,8,128]{4,3,2,1,0:T(8,128)(2,1)S(1)} custom-call(bf16[4,5,8,8,128]{4,3,2,1,0:T(8,128)(2,1)} %bitcast.5, bf16[27,4,256]{2,1,0:T(4,128)(2,1)} %bitcast.6, bf16[1,4]{1,0:T(2,128)(2,1)} %bitcast.7), custom_call_target="tpu_custom_call" | custom-call | flops 2264924160 | bytes 655360 | tf_op jit(solution)/shard_map/pallas_call | solution.py:417
  45.9 0.7 %copy.5 = bf16[4,5,64,128]{3,2,1,0:T(8,128)(2,1)} copy(bf16[4,5,64,128]{3,2,1,0:T(8,128)(2,1)S(1)} %bitcast.4) | data formatting | bytes 655360
